TPU v7x, 512 devices: a whole 4x4x16 slice. The times are simulated.
512 devices in a mesh: rep: 16 (over z), fsdp: 32 (over x, y, core).
Axes of the slice: x: 4, y: 4, z: 16, core: 2. Of those that a mesh axis runs over, the one named last changes fastest.
Arguments:
- gradient: bfloat16 [128, 1024, 1024], P(None, 'fsdp', 'rep')
- owner_slot: int32 [128], replicated, may hold values from 0 to 127, each once
- left_factor: bfloat16 [131072, 1024], P(('rep', 'fsdp'))
- right_factor: bfloat16 [131072, 1024], P(('rep', 'fsdp'))
- left_root: bfloat16 [131072, 1024], P(('rep', 'fsdp'))
- right_root: bfloat16 [131072, 1024], P(('rep', 'fsdp'))
Outputs:
- direction: bfloat16 [128, 1024, 1024], P(None, 'fsdp', 'rep')
- left_new: bfloat16 [131072, 1024], P(('rep', 'fsdp'))
- right_new: bfloat16 [131072, 1024], P(('rep', 'fsdp'))
Inputs may be any that keep to these rules, and one draw needn't show every extreme that they name: owner_slot names every slot of 0 to 127 exactly once.
All inputs are finite; a program needn't handle non-finite values.
Results may differ from a plain program's by a relative error of at most 0.0057.
Values may be sent and summed in bfloat16 or wider, within the bound.
A program may use at most 64 MiB of HBM per device.

v0:
```python
import jax
import jax.numpy as jnp
from jax import lax
from jax.sharding import PartitionSpec as P

B = 1024
GROUP = 4


BETA = 0.9
EPS = 1e-06


def partner(value, axis, apart):
    mask = 2**apart
    pairs = [(source, source ^ mask) for source in range(lax.axis_size(axis))]
    return lax.ppermute(value, axis, pairs)


def per_device(gradient, owner_slot, left_factor, right_factor, left_root, right_root):
    block_count = gradient.shape[0]
    row_width = gradient.shape[1]
    fsdp_count = lax.axis_size("fsdp")
    quarter = left_factor.shape[0]
    owners = fsdp_count // GROUP
    member = lax.axis_index("fsdp") % GROUP
    offset = member * quarter
    slot_ids = jnp.arange(block_count, dtype=jnp.int32)
    matches = (owner_slot[:, None] == slot_ids[None, :]).astype(jnp.int32)
    inverse = jnp.sum(matches * slot_ids[:, None], axis=0)
    arranged = jnp.take(gradient, inverse, axis=0)
    grouped = lax.all_to_all(arranged, "rep", split_axis=0, concat_axis=2, tiled=True)
    copies = jnp.repeat(grouped, GROUP, axis=0)
    whole_block = lax.all_to_all(copies, "fsdp", split_axis=0, concat_axis=0, tiled=True).reshape(
        B, B
    )
    column_part = lax.dynamic_slice_in_dim(whole_block, offset, quarter, 1)
    root_rows = left_root
    for bit_number in range(GROUP.bit_length() - 1):
        partner_rows = partner(root_rows, "fsdp", bit_number)
        upper_bit = lax.axis_index("fsdp") // 2**bit_number % 2
        root_rows = jnp.where(
            upper_bit == 1,
            jnp.concatenate((partner_rows, root_rows), axis=0),
            jnp.concatenate((root_rows, partner_rows), axis=0),
        )
    row_part = lax.dynamic_slice_in_dim(whole_block, offset, quarter, 0)
    gram_left = lax.dot_general(
        row_part, whole_block, (((1,), (1,)), ((), ())), preferred_element_type=jnp.float32
    )
    left_new = (BETA * left_factor.astype(jnp.float32) + (1.0 - BETA) / B * gram_left).astype(
        jnp.bfloat16
    )
    gram_right = lax.dot_general(
        column_part, whole_block, (((0,), (0,)), ((), ())), preferred_element_type=jnp.float32
    )
    right_new = (BETA * right_factor.astype(jnp.float32) + (1.0 - BETA) / B * gram_right).astype(
        jnp.bfloat16
    )
    right_half = lax.dot_general(
        whole_block, right_root, (((1,), (1,)), ((), ())), preferred_element_type=jnp.float32
    ).astype(jnp.bfloat16)
    precond = jnp.dot(root_rows, right_half, preferred_element_type=jnp.float32).astype(
        jnp.bfloat16
    )
    outgoing = precond.reshape(fsdp_count, row_width, quarter)
    returned = lax.all_to_all(outgoing, "fsdp", split_axis=0, concat_axis=0, tiled=True)
    rows_back = returned.reshape(owners, GROUP, row_width, quarter).transpose(0, 2, 1, 3)
    rows_back = rows_back.reshape(owners, row_width, B)
    spread_back = lax.all_to_all(rows_back, "rep", split_axis=2, concat_axis=0, tiled=True)
    local_dir = jnp.take(spread_back, owner_slot, axis=0)
    grad_local = jnp.sum(gradient.astype(jnp.float32) ** 2, axis=(1, 2))
    prec_local = jnp.sum(local_dir.astype(jnp.float32) ** 2, axis=(1, 2))
    grad_sq, prec_sq = lax.psum((grad_local, prec_local), ("rep", "fsdp"))
    ratio = jnp.sqrt((grad_sq + EPS) / (prec_sq + EPS))
    direction = (local_dir.astype(jnp.float32) * ratio[:, None, None]).astype(jnp.bfloat16)
    return (direction, left_new, right_new)


def solution(mesh):
    placed = (
        P(None, "fsdp", "rep"),
        P(),
        P(("rep", "fsdp"), None),
        P(("rep", "fsdp"), None),
        P(("rep", "fsdp"), None),
        P(("rep", "fsdp"), None),
    )
    return jax.shard_map(
        per_device,
        mesh=mesh,
        in_specs=placed,
        out_specs=(P(None, "fsdp", "rep"), P(("rep", "fsdp"), None), P(("rep", "fsdp"), None)),
        check_vma=False,
    )
```

profile of v0, /device:TPU:1, one launch (start us, length us, event | category | flops | bytes accessed | tf_op | source)
XLA Modules:
  0.0 286.8 jit_solution(2692289030630475650)
XLA Ops:
  0.6 0.0 copy-start
  0.6 0.8 select_reduce_fusion
  1.5 0.7 compare_select_fusion
  2.1 0.7 compare_and_fusion
  2.8 2.4 copy.24
  5.2 0.8 gather_fusion
  6.0 0.2 broadcast_select_fusion.1
  6.2 0.7 reshape.55
  7.0 38.4 %all_to_all.46 = bf16[16,2,8192]{2,1,0:T(2,128)(2,1)S(1)} all-to-all(bf16[16,2,8192]{2,1,0:T(2,128)(2,1)S(1)} %reshape.55), channel_id=1, replica_groups=mesh['rep'=16,'fsdp'=32] {'rep'}, dimensions={0} | all-to-all | bytes 1048576 | tf_op jit(solution)/shard_map/all_to_all | solution.py:32
  45.3 0.7 reshape.56
  46.0 0.7 copy.25
  46.7 0.7 all_to_all.35
  47.4 1.6 broadcast_in_dim.16
  49.0 0.0 copy-start.4
  49.0 14.4 %all-to-all-start.1 = ((bf16[32,32,1024]{2,1,0:T(8,128)(2,1)}), bf16[32,32,1024]{2,1,0:T(8,128)(2,1)S(1)}, u32[]{:S(2)}, u32[]{:S(2)}) async-start(bf16[32,32,1024]{2,1,0:T(8,128)(2,1)} %bitcast.2), calls=%async_computation.1 | async-start | bytes 4194304 | tf_op jit(solution)/shard_map/all_to_all | solution.py:34
  63.4 0.0 copy-done.4
  63.5 2.1 collective-permute-start
  65.6 1.8 collective-permute-done
  67.4 2.6 maximum_select_fusion.4
  70.0 3.3 %collective-permute-start.1 = (bf16[512,1024]{1,0:T(8,128)(2,1)}, bf16[512,1024]{1,0:T(8,128)(2,1)}, u32[]{:S(2)}, u32[]{:S(2)}) collective-permute-start(bf16[512,1024]{1,0:T(8,128)(2,1)} %maximum_select_fusion.4), channel_id=1, source_target_pairs={{0,2},{1,3},{2,0},{3,1},{4,6},{5,7},{6,4},{7,5},{8,10},{9,11},{10,... | collective-permute-start | bytes 3145736 | tf_op jit(solution)/shard_map/ppermute | solution.py:17
  73.4 37.5 %collective-permute-done.1 = bf16[512,1024]{1,0:T(8,128)(2,1)} collective-permute-done((bf16[512,1024]{1,0:T(8,128)(2,1)}, bf16[512,1024]{1,0:T(8,128)(2,1)}, u32[]{:S(2)}, u32[]{:S(2)}) %collective-permute-start.1) | collective-permute-done | bytes 1048608 | tf_op jit(solution)/shard_map/ppermute | solution.py:17
  110.9 0.0 all-to-all-done.1
  110.9 0.0 copy-start.2
  110.9 0.0 copy-done
  110.9 5.2 %fusion.13 = bf16[1024,256]{1,0:T(8,128)(2,1)S(1)} fusion(bf16[512,1024]{1,0:T(8,128)(2,1)} %maximum_select_fusion.4, bf16[512,1024]{1,0:T(8,128)(2,1)} %collective-permute-done.1, pred[]{:T(512)S(6)} %eq.23, bf16[1024,1024]{1,0:T(8,128)(2,1)S(1)} %bitcast.27, bf16[256,1024]{1,0:T(8,128)(2,1)S(1)} %copy-done), kind=kOutput, calls=%fused_computation.20 | convolution fusion | flops 1083703296 | bytes 5242881 | tf_op jit(solution)/shard_map/dot_general | solution.py:63
  116.1 0.0 copy-done.2
  116.1 18.7 %all_to_all.47 = bf16[32,32,256]{2,1,0:T(8,128)(2,1)S(1)} all-to-all(bf16[32,32,256]{2,1,0:T(8,128)(2,1)S(1)} %bitcast.30), channel_id=1, replica_groups=mesh['rep'=16,'fsdp'=32] {'fsdp'}, dimensions={0} | all-to-all | bytes 1048576 | tf_op jit(solution)/shard_map/all_to_all | solution.py:67
  134.8 1.2 copy.30
  135.9 0.0 copy-start.1
  136.0 2.7 reshape.57
  138.7 6.1 %all-to-all-start.3 = ((bf16[16,2,8192]{2,1,0:T(2,128)(2,1)}), bf16[16,2,8192]{2,1,0:T(2,128)(2,1)}, u32[]{:S(2)}, u32[]{:S(2)}) async-start(bf16[16,2,8192]{2,1,0:T(2,128)(2,1)} %reshape.57), calls=%async_computation.3 | async-start | bytes 1048576 | tf_op jit(solution)/shard_map/all_to_all | solution.py:70
  144.8 0.0 copy-done.1
  144.8 0.3 multiply_reduce_fusion
  145.1 0.0 copy-start.3
  145.1 0.0 copy-start.5
  145.1 3.6 %fusion.11 = bf16[256,1024]{1,0:T(8,128)(2,1)} fusion(bf16[1024,1024]{1,0:T(8,128)(2,1)} %bitcast.28, bf16[256,1024]{1,0:T(8,128)(2,1)} %param.10, s32[]{:T(128)S(6)} %select_n.55), kind=kOutput, calls=%fused_computation.18 | convolution fusion | flops 538181632 | bytes 3670020 | tf_op jit(solution)/shard_map/dot_general | solution.py:48
  148.7 0.0 copy-done.3
  148.7 0.0 copy-done.5
  148.7 1.6 fusion.12
  150.2 19.9 %all-to-all-done.3 = bf16[16,2,8192]{2,1,0:T(2,128)(2,1)} async-done(((bf16[16,2,8192]{2,1,0:T(2,128)(2,1)}), bf16[16,2,8192]{2,1,0:T(2,128)(2,1)}, u32[]{:S(2)}, u32[]{:S(2)}) %all-to-all-start.3) | async-done | bytes 524320 | tf_op jit(solution)/shard_map/all_to_all | solution.py:70
  170.1 3.1 %reshape.58 = bf16[1024,8,32]{2,1,0:T(8,128)(2,1)S(1)} reshape(bf16[16,2,8192]{2,1,0:T(2,128)(2,1)} %all-to-all-done.3) | data formatting | bytes 1048576
  173.2 1.9 copy.28
  175.1 2.0 gather_fusion.1
  177.1 2.0 fusion
  179.0 105.4 %all-reduce = (f32[128]{0:T(128)S(1)}, f32[128]{0:T(128)S(1)}) all-reduce(f32[128]{0:T(128)S(1)} %fusion, f32[128]{0:T(128)S(1)} %multiply_reduce_fusion), channel_id=1, replica_groups=mesh['rep'=16,'fsdp'=32] {'rep','fsdp'}, use_global_device_ids=true, to_apply=%region_4.6 | all-reduce | flops 256 | bytes 2048 | tf_op jit(solution)/shard_map/psum | solution.py:74
  284.5 0.4 fusion.1
  284.9 1.9 copy.29
  (3 shorter events, 0.0 us)
Async XLA Ops:
  0.6 110.2 %copy-start = (bf16[256,1024]{1,0:T(8,128)(2,1)S(1)}, bf16[256,1024]{1,0:T(8,128)(2,1)}, u32[]{:S(2)}) copy-start(bf16[256,1024]{1,0:T(8,128)(2,1)} %param.13) | copy-start | bytes 1572868
  49.0 14.5 %copy-start.4 = (bf16[256,1024]{1,0:T(8,128)(2,1)S(1)}, bf16[256,1024]{1,0:T(8,128)(2,1)}, u32[]{:S(2)}) copy-start(bf16[256,1024]{1,0:T(8,128)(2,1)} %param.12) | copy-start | bytes 1572868
  49.0 61.9 %all-to-all-start.1 = ((bf16[32,32,1024]{2,1,0:T(8,128)(2,1)}), bf16[32,32,1024]{2,1,0:T(8,128)(2,1)S(1)}, u32[]{:S(2)}, u32[]{:S(2)}) async-start(bf16[32,32,1024]{2,1,0:T(8,128)(2,1)} %bitcast.2), calls=%async_computation.1 | async-start | bytes 4194304 | tf_op jit(solution)/shard_map/all_to_all | solution.py:34
  63.5 3.9 %collective-permute-start = (bf16[256,1024]{1,0:T(8,128)(2,1)S(1)}, bf16[256,1024]{1,0:T(8,128)(2,1)}, u32[]{:S(2)}, u32[]{:S(2)}) collective-permute-start(bf16[256,1024]{1,0:T(8,128)(2,1)S(1)} %copy-done.4), channel_id=1, source_target_pairs={{0,1},{1,0},{2,3},{3,2},{4,5},{5,4},{6,7},{7,6},{8,9},{9,8},{10,11... | collective-permute-start | bytes 1572872 | tf_op jit(solution)/shard_map/ppermute | solution.py:17
  70.0 40.8 %collective-permute-start.1 = (bf16[512,1024]{1,0:T(8,128)(2,1)}, bf16[512,1024]{1,0:T(8,128)(2,1)}, u32[]{:S(2)}, u32[]{:S(2)}) collective-permute-start(bf16[512,1024]{1,0:T(8,128)(2,1)} %maximum_select_fusion.4), channel_id=1, source_target_pairs={{0,2},{1,3},{2,0},{3,1},{4,6},{5,7},{6,4},{7,5},{8,10},{9,11},{10,... | collective-permute-start | bytes 3145736 | tf_op jit(solution)/shard_map/ppermute | solution.py:17
  110.9 5.2 %copy-start.2 = (bf16[32,32,1024]{2,1,0:T(8,128)(2,1)}, bf16[32,32,1024]{2,1,0:T(8,128)(2,1)S(1)}, u32[]{:S(2)}) copy-start(bf16[32,32,1024]{2,1,0:T(8,128)(2,1)S(1)} %all-to-all-done.1) | copy-start | bytes 6291460
  135.9 8.8 %copy-start.1 = (bf16[128,32,64]{0,2,1:T(8,128)(2,1)S(1)}, bf16[128,32,64]{0,2,1:T(8,128)(2,1)}, u32[]{:S(2)}) copy-start(bf16[128,32,64]{0,2,1:T(8,128)(2,1)} %param.8) | copy-start | bytes 1572868
  138.7 31.4 %all-to-all-start.3 = ((bf16[16,2,8192]{2,1,0:T(2,128)(2,1)}), bf16[16,2,8192]{2,1,0:T(2,128)(2,1)}, u32[]{:S(2)}, u32[]{:S(2)}) async-start(bf16[16,2,8192]{2,1,0:T(2,128)(2,1)} %reshape.57), calls=%async_computation.3 | async-start | bytes 1048576 | tf_op jit(solution)/shard_map/all_to_all | solution.py:70
  145.1 3.6 %copy-start.3 = (bf16[32,32,1024]{2,1,0:T(8,128)(2,1)S(1)}, bf16[32,32,1024]{2,1,0:T(8,128)(2,1)}, u32[]{:S(2)}) copy-start(bf16[32,32,1024]{2,1,0:T(8,128)(2,1)} %copy-done.2) | copy-start | bytes 6291460
  145.1 3.6 %copy-start.5 = (bf16[256,1024]{1,0:T(8,128)(2,1)S(1)}, bf16[256,1024]{1,0:T(8,128)(2,1)}, u32[]{:S(2)}) copy-start(bf16[256,1024]{1,0:T(8,128)(2,1)} %param.11) | copy-start | bytes 1572868
where the time goes:
time: 287 us
  blocking collectives  162 us (56%)
  waiting for transfers between devices  59.2 us (21%)
  starting transfers between devices  25.9 us (9%)
  local copies, waits for them, and re-layouts  20.3 us (7%)
  matrix products  10.3 us (4%)
  other arithmetic  7.65 us (3%)
    psum x1, blocking collectives, per_device(): grad_sq, prec_sq = lax.psum((grad_local, prec_local), ('rep', 'fsdp'))  105 us
    ppermute x2, waiting for transfers between devices, partner(): return lax.ppermute(value, axis, pairs)  39.3 us
    all_to_all x1, blocking collectives, per_device(): lax.all_to_all(arranged, 'rep', split_axis=0, concat_axis=2, tiled=True)  38.4 us
    all_to_all x1, waiting for transfers between devices, per_device(): lax.all_to_all(rows_back, 'rep', split_axis=2, concat_axis=0, tiled=True)  19.9 us
    all_to_all x1, blocking collectives, per_device(): lax.all_to_all(outgoing, 'fsdp', split_axis=0, concat_axis=0, tiled=True)  18.7 us
    all_to_all x1, starting transfers between devices, per_device(): lax.all_to_all(copies, 'fsdp', split_axis=0, concat_axis=0, tiled=True)  14.4 us
    unnamed x18, local copies, waits for them, and re-layouts  11.5 us
    all_to_all x1, starting transfers between devices, per_device(): lax.all_to_all(rows_back, 'rep', split_axis=2, concat_axis=0, tiled=True)  6.08 us
  transfers between devices with their start and end apart: 4, of which 3 were waited for; matrix products, arithmetic and copies ran while one was open for 3% of the time, Pallas kernels for 0%

commit v1 on v0

v1 whole, which is shorter than its diff:
```python
import functools

import jax
import jax.numpy as jnp
from jax import lax
from jax.experimental import pallas as pl
from jax.experimental.pallas import tpu as pltpu
from jax.sharding import PartitionSpec as P

MESH = pl.DeviceIdType.MESH
F32 = jnp.float32
BF16 = jnp.bfloat16
B = 1024
GROUP = 4
BETA = 0.9
EPS = 1e-06
NZ = 16
NF = 32
NQ = NF // GROUP
QUARTER = B // GROUP
LANES = 128
NT = (((1,), (1,)), ((), ()))
TN = (((0,), (0,)), ((), ()))
STEPS = (1, -1, 2, -2, 3, -3, 4, -4, 5, -5, 6, -6, 7, -7, 8)


def halves(even, odd):
    lane = lax.broadcasted_iota(jnp.int32, even.shape, even.ndim - 1)
    low = lane < LANES // 2
    axis = even.ndim - 1
    top = jnp.where(low, even, pltpu.roll(odd, LANES // 2, axis))
    bottom = jnp.where(low, pltpu.roll(even, LANES // 2, axis), odd)
    return top, bottom


def kernel(
    owner_ref, grad_in, lf_in, rf_in, lr_in, rr_in,
    final, ln_out, rn_out,
    grad, wide, send_fwd, mid_fwd, raw, block, lroot, rroot, lfac, rfac,
    tpart, acc, pre, sums, send_back, mid_back, lnew, rnew,
    in_sem, out_sem, zf_s, zf_r, xf_s, xf_r, sib_s, sib_r, r_s, r_r,
    ex_s, ex_r, zb_s, zb_r, xb_s, xb_r,
):
    z = lax.axis_index("rep")
    f = lax.axis_index("fsdp")
    core = f % 2
    xy = f // 2
    m = f % GROUP
    own_q = f // GROUP
    x = f // 8
    zq = z // 4
    sibling = f + 1 - 2 * core
    across = f + 2 - 4 * (m // 2)
    m_across = m + 2 - 4 * (m // 2)
    near = 1 + 2 * (1 - (z % 4) // 2)
    quads = [zq, (zq + near) % 4, (zq + 4 - near) % 4, (zq + 2) % 4]

    def local(src, dst, sem):
        return pltpu.make_async_copy(src, dst, sem)

    def remote(src, dst, send, recv, zd, fd):
        return pltpu.make_async_remote_copy(
            src_ref=src, dst_ref=dst, send_sem=send, recv_sem=recv,
            device_id=(zd, fd), device_id_type=MESH,
        )

    def await_bytes(ref, sem):
        pltpu.make_async_copy(ref, ref, sem).wait()

    loads = [
        local(grad_in, grad, in_sem.at[0]),
        local(lr_in, lroot, in_sem.at[1]),
        local(rr_in, rroot.at[m], in_sem.at[2]),
        local(lf_in, lfac, in_sem.at[3]),
        local(rf_in, rfac, in_sem.at[4]),
    ]
    for load in loads:
        load.start()
    barrier = pltpu.get_barrier_semaphore()

    def greet_plane(i, carry):
        pl.semaphore_signal(barrier, inc=1, device_id=(z, (f + i) % NF), device_id_type=MESH)
        return carry

    def greet_ring(i, carry):
        pl.semaphore_signal(barrier, inc=1, device_id=((z + i) % NZ, f), device_id_type=MESH)
        return carry

    lax.fori_loop(1, NZ, greet_ring, 0)
    lax.fori_loop(1, NF, greet_plane, 0)

    owner = owner_ref[...]
    slot_row = lax.broadcasted_iota(jnp.int32, (LANES, LANES), 0)
    pick = (jnp.broadcast_to(owner, (LANES, LANES)) == slot_row).astype(BF16)
    loads[0].wait()
    for t in range(16):
        piece = jnp.concatenate((grad[t * 64 : t * 64 + 64, :], grad[(16 + t) * 64 : (16 + t) * 64 + 64, :]), axis=0)
        wide[pl.ds(t, LANES, stride=16), :] = lax.dot_general(pick, piece, NT, preferred_element_type=F32)
    for zd in range(NZ):
        send_fwd[zd] = wide[zd * 128 : zd * 128 + 128, :].reshape(NQ, 16, LANES).astype(BF16)

    pl.semaphore_wait(barrier, NZ - 1 + NF - 1)

    def send_z(zd):
        remote(send_fwd.at[zd], mid_fwd.at[z], zf_s, zf_r.at[z], zd, f).start()

    for step in STEPS:
        send_z((z + step + NZ) % NZ)
    local(send_fwd.at[z], mid_fwd.at[z], zf_r.at[z]).start()

    remote(rr_in, rroot.at[m], r_s.at[0], r_r.at[0], z, across).start()
    remote(rr_in, rroot.at[m], r_s.at[1], r_r.at[1], z, sibling).start()

    def forward_xy(qd):
        for t in range(4):
            await_bytes(mid_fwd.at[qd * 4 + t], zf_r.at[qd * 4 + t])

        def one(i, carry):
            q, chip = i // 2, i % 2
            fd = q * GROUP + chip * 2 + core
            src = mid_fwd.at[pl.ds(qd * 4, 4), q]
            dst = raw.at[xy, core, pl.ds(qd * 4, 4)]

            @pl.when(fd != f)
            def _():
                remote(src, dst, xf_s.at[qd], xf_r.at[qd], z, fd).start()

            @pl.when(fd == f)
            def _():
                local(src, dst, xf_r.at[qd]).start()

            return carry

        lax.fori_loop(0, 2 * NQ, one, 0)

    def share(qd):
        mine = raw.at[:, core, pl.ds(qd * 4, 4)]
        await_bytes(mine, xf_r.at[qd])
        remote(mine, mine, sib_s.at[qd], sib_r.at[qd], z, sibling).start()

    def gather_chunk(qd):
        await_bytes(raw.at[:, 1 - core, pl.ds(qd * 4, 4)], sib_r.at[qd])

        def unpack(i, carry):
            for pair in range(2):
                first = qd * 4 + 2 * pair
                even = raw[pl.ds(i * 2, 2), :, first].reshape(64, LANES)
                odd = raw[pl.ds(i * 2, 2), :, first + 1].reshape(64, LANES)
                top, bottom = halves(even, odd)
                rows = jnp.concatenate((top.reshape(4, 16, LANES), bottom.reshape(4, 16, LANES)), axis=1)
                at = pl.multiple_of(i * 128, 128)
                block[qd, pl.ds(at, 128), pair * LANES : (pair + 1) * LANES] = rows.reshape(128, LANES)
            return carry

        lax.fori_loop(0, NF // 4, unpack, 0)

    def left_product(qd):
        tpart[qd] = jnp.dot(lroot[...], block[qd], preferred_element_type=F32).astype(BF16)

    def right_product(qd, first=False, last=False):
        squares = jnp.zeros((8, LANES), F32)
        for j in range(GROUP):
            cols = slice(j * QUARTER, (j + 1) * QUARTER)
            part = lax.dot_general(
                tpart[qd], rroot[j, :, pl.ds(pl.multiple_of(qd * QUARTER, QUARTER), QUARTER)], NT,
                preferred_element_type=F32,
            )
            if first:
                acc[:, cols] = part
            elif not last:
                acc[:, cols] += part
            else:
                value = (acc[:, cols] + part).astype(BF16)
                pre[:, cols] = value
                wider = value.astype(F32)
                squares += jnp.sum((wider * wider).reshape(QUARTER // 8, 8, 2, LANES), axis=(0, 2))
        return squares

    def grad_squares(qd, total):
        rows = block[qd, pl.ds(pl.multiple_of(m * QUARTER, QUARTER), QUARTER), :].astype(F32)
        return total + jnp.sum((rows * rows).reshape(QUARTER // 8, 8, 2, LANES), axis=(0, 2))

    total = jnp.zeros((8, LANES), F32)
    forward_xy(quads[0])
    forward_xy(quads[1])
    loads[1].wait()
    share(quads[0])
    forward_xy(quads[2])
    share(quads[1])
    gather_chunk(quads[0])
    left_product(quads[0])
    total = grad_squares(quads[0], total)
    forward_xy(quads[3])
    await_bytes(rroot.at[m_across], r_r.at[0])
    remote(rroot.at[m_across], rroot.at[m_across], r_s.at[2], r_r.at[2], z, sibling).start()
    share(quads[2])
    gather_chunk(quads[1])
    left_product(quads[1])
    total = grad_squares(quads[1], total)
    loads[2].wait()
    await_bytes(rroot.at[0], r_r.at[1])
    await_bytes(rroot.at[0], r_r.at[2])
    right_product(quads[0], first=True)
    right_product(quads[1])
    share(quads[3])
    gather_chunk(quads[2])
    left_product(quads[2])
    total = grad_squares(quads[2], total)
    right_product(quads[2])
    gather_chunk(quads[3])
    left_product(quads[3])
    prec_total = right_product(quads[3], last=True)
    total = grad_squares(quads[3], total)

    sums[m, 0] = total
    sums[m, 1] = prec_total
    for step in range(1, GROUP):
        fd = own_q * GROUP + (m + step) % GROUP
        remote(sums.at[m], sums.at[m], ex_s.at[step - 1], ex_r.at[m], z, fd).start()
    for step in range(1, GROUP):
        await_bytes(sums.at[0], ex_r.at[(m + step) % GROUP])
    grad_sq = jnp.sum(sums[0, 0] + sums[1, 0] + sums[2, 0] + sums[3, 0], keepdims=True)
    prec_sq = jnp.sum(sums[0, 1] + sums[1, 1] + sums[2, 1] + sums[3, 1], keepdims=True)
    ratio = jnp.sqrt((grad_sq + EPS) / (prec_sq + EPS))

    def pack_quad(qd):
        for pair in range(2):
            col = pl.multiple_of(qd * QUARTER + pair * LANES, LANES)
            rows = (pre[:, pl.ds(col, LANES)].astype(F32) * ratio).astype(BF16).reshape(NQ, 2, 16, LANES)
            even, odd = halves(rows[:, 0].reshape(LANES, LANES), rows[:, 1].reshape(LANES, LANES))
            send_back[qd * 4 + 2 * pair] = even.reshape(NQ, 16, LANES)
            send_back[qd * 4 + 2 * pair + 1] = odd.reshape(NQ, 16, LANES)

    def send_z_back(zd):
        remote(send_back.at[zd], mid_back.at[z], zb_s, zb_r.at[z], zd, f).start()

    for qd in quads:
        pack_quad(qd)
    for step in STEPS:
        send_z_back((z + step + NZ) % NZ)
    local(send_back.at[z], mid_back.at[z], zb_r.at[z]).start()

    def back_xy(qd):
        for t in range(4):
            await_bytes(mid_back.at[qd * 4 + t], zb_r.at[qd * 4 + t])

        def one(d, carry):
            fd = m * NQ + d
            src = mid_back.at[pl.ds(qd * 4, 4), d]
            dst = final.at[own_q, pl.ds(qd * 4, 4)]

            @pl.when(fd != f)
            def _():
                remote(src, dst, xb_s.at[qd], xb_r.at[qd], z, fd).start()

            @pl.when(fd == f)
            def _():
                local(src, dst, xb_r.at[qd]).start()

            return carry

        lax.fori_loop(0, NQ, one, 0)

    def gram_left():
        rows = pl.ds(pl.multiple_of(m * QUARTER, QUARTER), QUARTER)
        for j in range(GROUP):
            gram = jnp.zeros((QUARTER, QUARTER), F32)
            for c in range(4):
                gram += lax.dot_general(
                    block[c, rows, :], block[c, j * QUARTER : (j + 1) * QUARTER, :], NT, preferred_element_type=F32
                )
            cols = slice(j * QUARTER, (j + 1) * QUARTER)
            lnew[:, cols] = (BETA * lfac[:, cols].astype(F32) + (1.0 - BETA) / B * gram).astype(BF16)

    def gram_right():
        for j in range(GROUP):
            gram = lax.dot_general(block[m], block[j], TN, preferred_element_type=F32)
            cols = slice(j * QUARTER, (j + 1) * QUARTER)
            rnew[:, cols] = (BETA * rfac[:, cols].astype(F32) + (1.0 - BETA) / B * gram).astype(BF16)

    loads[3].wait()
    gram_left()
    stores = [local(lnew, ln_out, out_sem.at[0]), local(rnew, rn_out, out_sem.at[1])]
    stores[0].start()
    back_xy(quads[0])
    loads[4].wait()
    gram_right()
    stores[1].start()
    back_xy(quads[1])
    back_xy(quads[2])
    back_xy(quads[3])

    for qd in quads:
        await_bytes(final.at[:, pl.ds(qd * 4, 4)], xb_r.at[qd])

    await_bytes(send_fwd.at[pl.ds(0, NZ - 1)], zf_s)
    await_bytes(send_back.at[pl.ds(0, NZ - 1)], zb_s)
    for c in range(4):
        await_bytes(raw.at[pl.ds(0, 15), 0, pl.ds(0, 4)], xf_s.at[c])
        await_bytes(raw.at[:, 0, pl.ds(0, 4)], sib_s.at[c])

        @pl.when(x == m)
        def _():
            await_bytes(final.at[pl.ds(0, NQ - 1), pl.ds(0, 4)], xb_s.at[c])

        @pl.when(x != m)
        def _():
            await_bytes(final.at[:, pl.ds(0, 4)], xb_s.at[c])

    for i in range(3):
        await_bytes(rroot.at[0], r_s.at[i])
        await_bytes(sums.at[0], ex_s.at[i])
    stores[0].wait()
    stores[1].wait()


def finish(owner_ref, final, lnew, rnew, dir_out, ln_out, rn_out, rows_in, wide, dirv, lvmem, rvmem, in_sem, out_sem):
    loads = [pltpu.make_async_copy(final.at[q], rows_in.at[q], in_sem.at[q]) for q in range(NQ)]
    stores = [
        pltpu.make_async_copy(lvmem, ln_out, out_sem.at[0]),
        pltpu.make_async_copy(rvmem, rn_out, out_sem.at[1]),
        pltpu.make_async_copy(dirv, dir_out, out_sem.at[2]),
    ]
    loads.append(pltpu.make_async_copy(lnew, lvmem, in_sem.at[NQ]))
    loads.append(pltpu.make_async_copy(rnew, rvmem, in_sem.at[NQ + 1]))
    for copy in loads:
        copy.start()
    row = lax.broadcasted_iota(jnp.int32, (LANES, LANES), 0)
    slot_of = (row % NZ) * NQ + row // NZ
    place = (jnp.broadcast_to(owner_ref[...], (LANES, LANES)) == slot_of).astype(BF16)
    for q in range(NQ):
        loads[q].wait()
        wide[q * 256 : q * 256 + 256, :] = rows_in[q].reshape(256, LANES).astype(F32)
    for i in range(2):
        loads[NQ + i].wait()
        stores[i].start()
    for t in range(16):
        rows = wide[pl.ds(t, LANES, stride=16), :].astype(BF16)
        blocks = lax.dot_general(rows, place, TN, preferred_element_type=F32).astype(BF16)
        dirv[t * 64 : t * 64 + 64, :] = blocks[:64]
        dirv[(16 + t) * 64 : (16 + t) * 64 + 64, :] = blocks[64:]
    stores[2].start()
    for copy in stores:
        copy.wait()


def per_device(gradient, owner_slot, left_factor, right_factor, left_root, right_root):
    blocks, row_width, col_width = gradient.shape
    columns = gradient.transpose(1, 2, 0).reshape(row_width * col_width, blocks)
    anywhere = pl.BlockSpec(memory_space=pl.ANY)
    factor = jax.ShapeDtypeStruct((QUARTER, B), BF16)
    dma = pltpu.SemaphoreType.DMA
    owner = owner_slot.reshape(1, blocks)
    final, left_new, right_new = pl.pallas_call(
        kernel,
        out_shape=(jax.ShapeDtypeStruct((NQ, NZ, 16, LANES), BF16), factor, factor),
        in_specs=[pl.BlockSpec(memory_space=pltpu.VMEM)] + [anywhere] * 5,
        out_specs=(anywhere, anywhere, anywhere),
        scratch_shapes=[
            pltpu.VMEM((2048, LANES), BF16),
            pltpu.VMEM((2048, LANES), F32),
            pltpu.VMEM((NZ, NQ, 16, LANES), BF16),
            pltpu.VMEM((NZ, NQ, 16, LANES), BF16),
            pltpu.VMEM((NF // 2, 2, NZ, 16, LANES), BF16),
            pltpu.VMEM((4, B, QUARTER), BF16),
            pltpu.VMEM((QUARTER, B), BF16),
            pltpu.VMEM((GROUP, QUARTER, B), BF16),
            pltpu.VMEM((QUARTER, B), BF16),
            pltpu.VMEM((QUARTER, B), BF16),
            pltpu.VMEM((4, QUARTER, QUARTER), BF16),
            pltpu.VMEM((QUARTER, B), F32),
            pltpu.VMEM((QUARTER, B), BF16),
            pltpu.VMEM((GROUP, 2, 8, LANES), F32),
            pltpu.VMEM((NZ, NQ, 16, LANES), BF16),
            pltpu.VMEM((NZ, NQ, 16, LANES), BF16),
            pltpu.VMEM((QUARTER, B), BF16),
            pltpu.VMEM((QUARTER, B), BF16),
            dma((5,)), dma((2,)),
            dma, dma((NZ,)),
            dma((4,)), dma((4,)),
            dma((4,)), dma((4,)),
            dma((3,)), dma((3,)),
            dma((3,)), dma((GROUP,)),
            dma, dma((NZ,)),
            dma((4,)), dma((4,)),
        ],
        compiler_params=pltpu.CompilerParams(
            collective_id=0, has_side_effects=True, vmem_limit_bytes=60 * 1024 * 1024
        ),
        cost_estimate=pl.CostEstimate(flops=2_200_000_000, bytes_accessed=8_000_000, transcendentals=0),
    )(owner, columns, left_factor, right_factor, left_root, right_root)
    direction, left_new, right_new = pl.pallas_call(
        finish,
        out_shape=(jax.ShapeDtypeStruct(columns.shape, BF16), factor, factor),
        in_specs=[pl.BlockSpec(memory_space=pltpu.VMEM)] + [anywhere] * 3,
        out_specs=(anywhere, anywhere, anywhere),
        scratch_shapes=[
            pltpu.VMEM((NQ, NZ, 16, LANES), BF16),
            pltpu.VMEM((2048, LANES), F32),
            pltpu.VMEM((2048, LANES), BF16),
            pltpu.VMEM((QUARTER, B), BF16),
            pltpu.VMEM((QUARTER, B), BF16),
            dma((NQ + 2,)),
            dma((3,)),
        ],
        compiler_params=pltpu.CompilerParams(vmem_limit_bytes=60 * 1024 * 1024),
        cost_estimate=pl.CostEstimate(flops=70_000_000, bytes_accessed=4_000_000, transcendentals=0),
    )(owner, final, left_new, right_new)
    return direction.reshape(row_width, col_width, blocks).transpose(2, 0, 1), left_new, right_new


def solution(mesh):
    placed = (
        P(None, "fsdp", "rep"),
        P(),
        P(("rep", "fsdp"), None),
        P(("rep", "fsdp"), None),
        P(("rep", "fsdp"), None),
        P(("rep", "fsdp"), None),
    )
    return jax.shard_map(
        per_device,
        mesh=mesh,
        in_specs=placed,
        out_specs=(P(None, "fsdp", "rep"), P(("rep", "fsdp"), None), P(("rep", "fsdp"), None)),
        check_vma=False,
    )
```

time: 287 us -> 97.1 us (0.34)
  blocking collectives: 162 us -> 0 us
  Pallas kernels: 0 us -> 96.2 us
  waiting for transfers between devices: 59.2 us -> 0 us
  starting transfers between devices: 25.9 us -> 0 us
  local copies, waits for them, and re-layouts: 20.3 us -> 0 us
  matrix products: 10.3 us -> 0 us
  other arithmetic: 7.65 us -> 0 us
    psum x1 -> x0, blocking collectives: 105 us -> none  [per_device(): grad_sq, prec_sq = lax.psum((grad_local, prec_local), ('rep', 'fsdp'))]
    pallas_call x0 -> x2, Pallas kernels: none -> 96.2 us  [the longest x1 92.7 us: per_device(): pl.pallas_call(kernel, out_shape=(jax.ShapeDtypeStruct((NQ, NZ, 16, LANES...]
    all_to_all x2 -> x0, blocking collectives: 57 us -> none  [the longest x1 38.4 us: per_device(): lax.all_to_all(arranged, 'rep', split_axis=0, concat_axis=2, tiled=True)]
    ppermute x2 -> x0, waiting for transfers between devices: 39.3 us -> none  [partner(): return lax.ppermute(value, axis, pairs)]
    all_to_all x2 -> x0, starting transfers between devices: 20.5 us -> none  [the longest x1 14.4 us: per_device(): lax.all_to_all(copies, 'fsdp', split_axis=0, concat_axis=0, tiled=True)]
    all_to_all x2 -> x0, waiting for transfers between devices: 19.9 us -> none  [the longest x1 19.9 us: per_device(): lax.all_to_all(rows_back, 'rep', split_axis=2, concat_axis=0, tiled=True)]
    unnamed x18 -> x0, local copies, waits for them, and re-layouts: 11.5 us -> none
    dot_general x3 -> x0, matrix products: 10.3 us -> none  [the longest x1 5.19 us: per_device(): jnp.dot(root_rows, right_half, preferred_element_type=jnp.float32)]
  transfers between devices with their start and end apart: 4 -> 0, of which waited for: 3 -> 0; matrix products, arithmetic and copies ran while one was open for 3% -> 0% of each run, Pallas kernels for 0% -> 0%
where the time goes in v1:
time: 97.1 us; the launch traced here: 96.9 us
  Pallas kernels  96.2 us (99%)
    pallas_call x1, Pallas kernels, per_device(): pl.pallas_call(kernel, out_shape=(jax.ShapeDtypeStruct((NQ, NZ, 16, LANES...  92.7 us
    pallas_call x1, Pallas kernels, per_device(): pl.pallas_call(finish, out_shape=(jax.ShapeDtypeStruct(columns.shape, BF1...  3.57 us

profile of v1, /device:TPU:1, one launch (start us, length us, event | category | flops | bytes accessed | tf_op | source)
XLA Modules:
  0.0 96.9 jit_solution(12413789765496460363)
XLA Ops:
  0.6 92.7 %shard_map.85 = (bf16[8,16,16,128]{3,2,1,0:T(8,128)(2,1)}, bf16[256,1024]{1,0:T(8,128)(2,1)}, bf16[256,1024]{1,0:T(8,128)(2,1)}) custom-call(s32[1,128]{1,0:T(1,128)} %bitcast.7, bf16[2048,128]{1,0:T(8,128)(2,1)} %bitcast.9, bf16[256,1024]{1,0:T(8,128)(2,1)} %lf_in.1, bf16[256,1024]{1,0:T(8,128)(2,1)} %rf_in.1, bf16[256,1024]{1,0:T(8,128)(2,1)} %lr_in.1, ...), custom_call_target="tpu_custom_call" | custom-call | flops 2200000000 | bytes 8000000 | tf_op jit(solution)/shard_map/pallas_call | solution.py:354
  93.3 3.6 %shard_map.86 = (bf16[2048,128]{1,0:T(8,128)(2,1)}, bf16[256,1024]{1,0:T(8,128)(2,1)}, bf16[256,1024]{1,0:T(8,128)(2,1)}) custom-call(s32[1,128]{1,0:T(1,128)} %bitcast.8, bf16[8,16,16,128]{3,2,1,0:T(8,128)(2,1)} %get-tuple-element.9.final, bf16[256,1024]{1,0:T(8,128)(2,1)} %get-tuple-element.10.lnew, bf16[256,1024]{1,0:T(8,128)(2,1)} %get-tuple-element.11.rnew), custom_call_target="tpu_custom_call" | custom-call | flops 70000000 | bytes 4000000 | tf_op jit(solution)/shard_map/pallas_call | solution.py:392

commit v2 on v1

--- a/solution.py
+++ b/solution.py
@@ -21,9 +21,6 @@
 LANES = 128
 NT = (((1,), (1,)), ((), ()))
 TN = (((0,), (0,)), ((), ()))
-STEPS = (1, -1, 2, -2, 3, -3, 4, -4, 5, -5, 6, -6, 7, -7, 8)
-
-
 def halves(even, odd):
     lane = lax.broadcasted_iota(jnp.int32, even.shape, even.ndim - 1)
     low = lane < LANES // 2
@@ -37,9 +34,9 @@
     owner_ref, grad_in, lf_in, rf_in, lr_in, rr_in,
     final, ln_out, rn_out,
     grad, wide, send_fwd, mid_fwd, raw, block, lroot, rroot, lfac, rfac,
-    tpart, acc, pre, sums, send_back, mid_back, lnew, rnew,
+    tpart, acc, gains, sums, send_back, mid_back, lnew, rnew, stop_fwd, stop_back,
     in_sem, out_sem, zf_s, zf_r, xf_s, xf_r, sib_s, sib_r, r_s, r_r,
-    ex_s, ex_r, zb_s, zb_r, xb_s, xb_r,
+    ex_s, ex_r, gain_s, gain_r, zb_s, zb_r, xb_s, xb_r, stop_r,
 ):
     z = lax.axis_index("rep")
     f = lax.axis_index("fsdp")
@@ -101,42 +98,58 @@
 
     pl.semaphore_wait(barrier, NZ - 1 + NF - 1)
 
-    def send_z(zd):
-        remote(send_fwd.at[zd], mid_fwd.at[z], zf_s, zf_r.at[z], zd, f).start()
-
-    for step in STEPS:
-        send_z((z + step + NZ) % NZ)
+    way = 1 - 2 * core
+
+    def send_z(send, mid, send_sem, recv_sem, step):
+        zd = (z + step * way + NZ) % NZ
+        remote(send.at[zd], mid.at[z], send_sem, recv_sem.at[z], zd, f).start()
+
+    def send_stop(send, stop, send_sem, recv_sem):
+        zd = (z + way + NZ) % NZ
+        remote(send.at[(z + NZ // 2) % NZ], stop, send_sem, recv_sem, zd, f).start()
+
+    def pass_stop(mid, stop, send_sem, stop_sem, recv_sem):
+        await_bytes(stop, stop_sem)
+        origin = (z - way + NZ) % NZ
+        zd = (z + 7 * way + NZ) % NZ
+        remote(stop, mid.at[origin], send_sem, recv_sem.at[origin], zd, f).start()
+
+    def send_root(member, index, fd, parts):
+        for part in parts:
+            rows = rroot.at[member, pl.ds(part * 64, 64)]
+            remote(rows, rows, r_s.at[index], r_r.at[index], z, fd).start()
+
+    loads[2].wait()
+    send_stop(send_fwd, stop_fwd, zf_s, stop_r.at[0])
+    for step in range(1, 6):
+        for sign in (1, -1):
+            send_z(send_fwd, mid_fwd, zf_s, zf_r, sign * step)
+        if step < 5:
+            send_root(m, 0, across, (step - 1,))
     local(send_fwd.at[z], mid_fwd.at[z], zf_r.at[z]).start()
-
-    remote(rr_in, rroot.at[m], r_s.at[0], r_r.at[0], z, across).start()
-    remote(rr_in, rroot.at[m], r_s.at[1], r_r.at[1], z, sibling).start()
+    send_root(m, 1, sibling, range(4))
+    pass_stop(mid_fwd, stop_fwd, zf_s, stop_r.at[0], zf_r)
 
     def forward_xy(qd):
         for t in range(4):
             await_bytes(mid_fwd.at[qd * 4 + t], zf_r.at[qd * 4 + t])
 
-        def one(i, carry):
-            q, chip = i // 2, i % 2
-            fd = q * GROUP + chip * 2 + core
+        for i in range(NF // 2):
+            chip = (xy + i) % (NF // 2)
+            q = chip // 2
             src = mid_fwd.at[pl.ds(qd * 4, 4), q]
             dst = raw.at[xy, core, pl.ds(qd * 4, 4)]
-
-            @pl.when(fd != f)
-            def _():
-                remote(src, dst, xf_s.at[qd], xf_r.at[qd], z, fd).start()
-
-            @pl.when(fd == f)
-            def _():
-                local(src, dst, xf_r.at[qd]).start()
-
-            return carry
-
-        lax.fori_loop(0, 2 * NQ, one, 0)
+            if i == 0:
+                local(src, dst, xf_r.at[qd, x]).start()
+            else:
+                remote(src, dst, xf_s.at[qd], xf_r.at[qd, x], z, chip * 2 + core).start()
 
     def share(qd):
-        mine = raw.at[:, core, pl.ds(qd * 4, 4)]
-        await_bytes(mine, xf_r.at[qd])
-        remote(mine, mine, sib_s.at[qd], sib_r.at[qd], z, sibling).start()
+        for i in range(4):
+            column = (x + i) % 4
+            mine = raw.at[pl.ds(column * 4, 4), core, pl.ds(qd * 4, 4)]
+            await_bytes(mine, xf_r.at[qd, column])
+            remote(mine, mine, sib_s.at[qd], sib_r.at[qd], z, sibling).start()
 
     def gather_chunk(qd):
         await_bytes(raw.at[:, 1 - core, pl.ds(qd * 4, 4)], sib_r.at[qd])
@@ -157,24 +170,18 @@
     def left_product(qd):
         tpart[qd] = jnp.dot(lroot[...], block[qd], preferred_element_type=F32).astype(BF16)
 
-    def right_product(qd, first=False, last=False):
-        squares = jnp.zeros((8, LANES), F32)
+    def right_part(qd, j):
+        return lax.dot_general(
+            tpart[qd], rroot[j, :, pl.ds(pl.multiple_of(qd * QUARTER, QUARTER), QUARTER)], NT,
+            preferred_element_type=F32,
+        )
+
+    def right_product(qd, first=False):
         for j in range(GROUP):
-            cols = slice(j * QUARTER, (j + 1) * QUARTER)
-            part = lax.dot_general(
-                tpart[qd], rroot[j, :, pl.ds(pl.multiple_of(qd * QUARTER, QUARTER), QUARTER)], NT,
-                preferred_element_type=F32,
-            )
             if first:
-                acc[:, cols] = part
-            elif not last:
-                acc[:, cols] += part
+                acc[j] = right_part(qd, j)
             else:
-                value = (acc[:, cols] + part).astype(BF16)
-                pre[:, cols] = value
-                wider = value.astype(F32)
-                squares += jnp.sum((wider * wider).reshape(QUARTER // 8, 8, 2, LANES), axis=(0, 2))
-        return squares
+                acc[j] += right_part(qd, j)
 
     def grad_squares(qd, total):
         rows = block[qd, pl.ds(pl.multiple_of(m * QUARTER, QUARTER), QUARTER), :].astype(F32)
@@ -182,6 +189,9 @@
 
     total = jnp.zeros((8, LANES), F32)
     forward_xy(quads[0])
+    for step in (6, 7):
+        for sign in (1, -1):
+            send_z(send_fwd, mid_fwd, zf_s, zf_r, sign * step)
     forward_xy(quads[1])
     loads[1].wait()
     share(quads[0])
@@ -190,14 +200,13 @@
     gather_chunk(quads[0])
     left_product(quads[0])
     total = grad_squares(quads[0], total)
+    await_bytes(rroot.at[m_across], r_r.at[0])
+    send_root(m_across, 2, sibling, range(4))
     forward_xy(quads[3])
-    await_bytes(rroot.at[m_across], r_r.at[0])
-    remote(rroot.at[m_across], rroot.at[m_across], r_s.at[2], r_r.at[2], z, sibling).start()
     share(quads[2])
     gather_chunk(quads[1])
     left_product(quads[1])
     total = grad_squares(quads[1], total)
-    loads[2].wait()
     await_bytes(rroot.at[0], r_r.at[1])
     await_bytes(rroot.at[0], r_r.at[2])
     right_product(quads[0], first=True)
@@ -209,57 +218,67 @@
     right_product(quads[2])
     gather_chunk(quads[3])
     left_product(quads[3])
-    prec_total = right_product(quads[3], last=True)
-    total = grad_squares(quads[3], total)
-
-    sums[m, 0] = total
+
+    prec_total = jnp.zeros((8, LANES), F32)
+    for c in range(4):
+        value = (acc[c] + right_part(quads[3], c)).astype(BF16)
+        for pair in range(2):
+            rows = value[:, pair * LANES : (pair + 1) * LANES].reshape(NQ, 2, 16, LANES)
+            even, odd = halves(rows[:, 0].reshape(LANES, LANES), rows[:, 1].reshape(LANES, LANES))
+            send_back[c * 4 + 2 * pair] = even.reshape(NQ, 16, LANES)
+            send_back[c * 4 + 2 * pair + 1] = odd.reshape(NQ, 16, LANES)
+        wider = value.astype(F32)
+        prec_total += jnp.sum((wider * wider).reshape(QUARTER // 8, 8, 2, LANES), axis=(0, 2))
+
+    sums[m, 0] = grad_squares(quads[3], total)
     sums[m, 1] = prec_total
     for step in range(1, GROUP):
         fd = own_q * GROUP + (m + step) % GROUP
         remote(sums.at[m], sums.at[m], ex_s.at[step - 1], ex_r.at[m], z, fd).start()
+    send_stop(send_back, stop_back, zb_s, stop_r.at[1])
+    for step in (1, 2, 3):
+        for sign in (1, -1):
+            send_z(send_back, mid_back, zb_s, zb_r, sign * step)
+    local(send_back.at[z], mid_back.at[z], zb_r.at[z]).start()
     for step in range(1, GROUP):
         await_bytes(sums.at[0], ex_r.at[(m + step) % GROUP])
     grad_sq = jnp.sum(sums[0, 0] + sums[1, 0] + sums[2, 0] + sums[3, 0], keepdims=True)
     prec_sq = jnp.sum(sums[0, 1] + sums[1, 1] + sums[2, 1] + sums[3, 1], keepdims=True)
-    ratio = jnp.sqrt((grad_sq + EPS) / (prec_sq + EPS))
-
-    def pack_quad(qd):
-        for pair in range(2):
-            col = pl.multiple_of(qd * QUARTER + pair * LANES, LANES)
-            rows = (pre[:, pl.ds(col, LANES)].astype(F32) * ratio).astype(BF16).reshape(NQ, 2, 16, LANES)
-            even, odd = halves(rows[:, 0].reshape(LANES, LANES), rows[:, 1].reshape(LANES, LANES))
-            send_back[qd * 4 + 2 * pair] = even.reshape(NQ, 16, LANES)
-            send_back[qd * 4 + 2 * pair + 1] = odd.reshape(NQ, 16, LANES)
-
-    def send_z_back(zd):
-        remote(send_back.at[zd], mid_back.at[z], zb_s, zb_r.at[z], zd, f).start()
-
-    for qd in quads:
-        pack_quad(qd)
-    for step in STEPS:
-        send_z_back((z + step + NZ) % NZ)
-    local(send_back.at[z], mid_back.at[z], zb_r.at[z]).start()
+    gains[z] = jnp.broadcast_to(jnp.sqrt((grad_sq + EPS) / (prec_sq + EPS)), (1, LANES))
+    for step in range(1, NZ):
+        zd = (z + step) % NZ
+        remote(gains.at[z], gains.at[z], gain_s, gain_r.at[z], zd, f).start()
+    for step in (4, 5, 6, 7):
+        for sign in (1, -1):
+            send_z(send_back, mid_back, zb_s, zb_r, sign * step)
+    pass_stop(mid_back, stop_back, zb_s, stop_r.at[1], zb_r)
 
     def back_xy(qd):
         for t in range(4):
-            await_bytes(mid_back.at[qd * 4 + t], zb_r.at[qd * 4 + t])
-
-        def one(d, carry):
+            zs = qd * 4 + t
+            await_bytes(mid_back.at[zs], zb_r.at[zs])
+
+            @pl.when(zs != z)
+            def _():
+                await_bytes(gains.at[zs], gain_r.at[zs])
+
+            mid_back[zs] = (mid_back[zs].astype(F32) * gains[zs].reshape(1, 1, LANES)).astype(BF16)
+        for i in range(NQ):
+            d = (f % NQ + i) % NQ
             fd = m * NQ + d
             src = mid_back.at[pl.ds(qd * 4, 4), d]
             dst = final.at[own_q, pl.ds(qd * 4, 4)]
-
-            @pl.when(fd != f)
+            if i > 0:
+                remote(src, dst, xb_s.at[qd], xb_r.at[qd], z, fd).start()
+                continue
+
+            @pl.when(x != m)
             def _():
                 remote(src, dst, xb_s.at[qd], xb_r.at[qd], z, fd).start()
 
-            @pl.when(fd == f)
+            @pl.when(x == m)
             def _():
                 local(src, dst, xb_r.at[qd]).start()
-
-            return carry
-
-        lax.fori_loop(0, NQ, one, 0)
 
     def gram_left():
         rows = pl.ds(pl.multiple_of(m * QUARTER, QUARTER), QUARTER)
@@ -293,8 +312,8 @@
     for qd in quads:
         await_bytes(final.at[:, pl.ds(qd * 4, 4)], xb_r.at[qd])
 
-    await_bytes(send_fwd.at[pl.ds(0, NZ - 1)], zf_s)
-    await_bytes(send_back.at[pl.ds(0, NZ - 1)], zb_s)
+    await_bytes(send_fwd, zf_s)
+    await_bytes(send_back, zb_s)
     for c in range(4):
         await_bytes(raw.at[pl.ds(0, 15), 0, pl.ds(0, 4)], xf_s.at[c])
         await_bytes(raw.at[:, 0, pl.ds(0, 4)], sib_s.at[c])
@@ -307,6 +326,7 @@
         def _():
             await_bytes(final.at[:, pl.ds(0, 4)], xb_s.at[c])
 
+    await_bytes(gains.at[pl.ds(0, NZ - 1)], gain_s)
     for i in range(3):
         await_bytes(rroot.at[0], r_s.at[i])
         await_bytes(sums.at[0], ex_s.at[i])
@@ -368,21 +388,25 @@
             pltpu.VMEM((QUARTER, B), BF16),
             pltpu.VMEM((QUARTER, B), BF16),
             pltpu.VMEM((4, QUARTER, QUARTER), BF16),
-            pltpu.VMEM((QUARTER, B), F32),
-            pltpu.VMEM((QUARTER, B), BF16),
+            pltpu.VMEM((GROUP, QUARTER, QUARTER), F32),
+            pltpu.VMEM((NZ, 1, LANES), F32),
             pltpu.VMEM((GROUP, 2, 8, LANES), F32),
             pltpu.VMEM((NZ, NQ, 16, LANES), BF16),
             pltpu.VMEM((NZ, NQ, 16, LANES), BF16),
             pltpu.VMEM((QUARTER, B), BF16),
             pltpu.VMEM((QUARTER, B), BF16),
+            pltpu.VMEM((NQ, 16, LANES), BF16),
+            pltpu.VMEM((NQ, 16, LANES), BF16),
             dma((5,)), dma((2,)),
             dma, dma((NZ,)),
-            dma((4,)), dma((4,)),
+            dma((4,)), dma((4, 4)),
             dma((4,)), dma((4,)),
             dma((3,)), dma((3,)),
             dma((3,)), dma((GROUP,)),
             dma, dma((NZ,)),
+            dma, dma((NZ,)),
             dma((4,)), dma((4,)),
+            dma((2,)),
         ],
         compiler_params=pltpu.CompilerParams(
             collective_id=0, has_side_effects=True, vmem_limit_bytes=60 * 1024 * 1024

time: 97.1 us -> 95.3 us (0.981)
  Pallas kernels: 96.2 us -> 94.5 us
    pallas_call x1, Pallas kernels: 92.7 us -> 90.9 us  [per_device(): pl.pallas_call(kernel, out_shape=(jax.ShapeDtypeStruct((NQ, NZ, 16, LANES...]
where the time goes in v2:
time: 95.3 us; the launch traced here: 95.1 us
  Pallas kernels  94.5 us (99%)
    pallas_call x1, Pallas kernels, per_device(): pl.pallas_call(kernel, out_shape=(jax.ShapeDtypeStruct((NQ, NZ, 16, LANES...  90.9 us
    pallas_call x1, Pallas kernels, per_device(): pl.pallas_call(finish, out_shape=(jax.ShapeDtypeStruct(columns.shape, BF1...  3.57 us

profile of v2, /device:TPU:1, one launch (start us, length us, event | category | flops | bytes accessed | tf_op | source)
XLA Modules:
  0.0 95.1 jit_solution(3067479937358796802)
XLA Ops:
  0.6 90.9 %shard_map.85 = (bf16[8,16,16,128]{3,2,1,0:T(8,128)(2,1)}, bf16[256,1024]{1,0:T(8,128)(2,1)}, bf16[256,1024]{1,0:T(8,128)(2,1)}) custom-call(s32[1,128]{1,0:T(1,128)} %bitcast.7, bf16[2048,128]{1,0:T(8,128)(2,1)} %bitcast.9, bf16[256,1024]{1,0:T(8,128)(2,1)} %lf_in.1, bf16[256,1024]{1,0:T(8,128)(2,1)} %rf_in.1, bf16[256,1024]{1,0:T(8,128)(2,1)} %lr_in.1, ...), custom_call_target="tpu_custom_call" | custom-call | flops 2200000000 | bytes 8000000 | tf_op jit(solution)/shard_map/pallas_call | solution.py:374
  91.6 3.6 %shard_map.86 = (bf16[2048,128]{1,0:T(8,128)(2,1)}, bf16[256,1024]{1,0:T(8,128)(2,1)}, bf16[256,1024]{1,0:T(8,128)(2,1)}) custom-call(s32[1,128]{1,0:T(1,128)} %bitcast.8, bf16[8,16,16,128]{3,2,1,0:T(8,128)(2,1)} %get-tuple-element.9.final, bf16[256,1024]{1,0:T(8,128)(2,1)} %get-tuple-element.10.lnew, bf16[256,1024]{1,0:T(8,128)(2,1)} %get-tuple-element.11.rnew), custom_call_target="tpu_custom_call" | custom-call | flops 70000000 | bytes 4000000 | tf_op jit(solution)/shard_map/pallas_call | solution.py:416

commit v3 on v2

--- a/solution.py
+++ b/solution.py
@@ -101,18 +101,21 @@
     way = 1 - 2 * core
 
     def send_z(send, mid, send_sem, recv_sem, step):
-        zd = (z + step * way + NZ) % NZ
-        remote(send.at[zd], mid.at[z], send_sem, recv_sem.at[z], zd, f).start()
+        if step > 2:
+            await_bytes(send.at[pl.ds(0, 2)], send_sem.at[step - 2])
+        for sign in (1, -1):
+            zd = (z + sign * step * way + NZ) % NZ
+            remote(send.at[zd], mid.at[z], send_sem.at[step], recv_sem.at[z], zd, f).start()
 
     def send_stop(send, stop, send_sem, recv_sem):
         zd = (z + way + NZ) % NZ
-        remote(send.at[(z + NZ // 2) % NZ], stop, send_sem, recv_sem, zd, f).start()
+        remote(send.at[(z + NZ // 2) % NZ], stop, send_sem.at[0], recv_sem, zd, f).start()
 
     def pass_stop(mid, stop, send_sem, stop_sem, recv_sem):
         await_bytes(stop, stop_sem)
         origin = (z - way + NZ) % NZ
         zd = (z + 7 * way + NZ) % NZ
-        remote(stop, mid.at[origin], send_sem, recv_sem.at[origin], zd, f).start()
+        remote(stop, mid.at[origin], send_sem.at[0], recv_sem.at[origin], zd, f).start()
 
     def send_root(member, index, fd, parts):
         for part in parts:
@@ -120,15 +123,25 @@
             remote(rows, rows, r_s.at[index], r_r.at[index], z, fd).start()
 
     loads[2].wait()
+    def hop_fwd(step):
+        send_z(send_fwd, mid_fwd, zf_s, zf_r, step)
+
+    def hop_back(step):
+        send_z(send_back, mid_back, zb_s, zb_r, step)
+
     send_stop(send_fwd, stop_fwd, zf_s, stop_r.at[0])
-    for step in range(1, 6):
-        for sign in (1, -1):
-            send_z(send_fwd, mid_fwd, zf_s, zf_r, sign * step)
-        if step < 5:
-            send_root(m, 0, across, (step - 1,))
+    hop_fwd(1)
+    send_root(m, 0, across, (0,))
+    hop_fwd(2)
+    send_root(m, 0, across, (1,))
     local(send_fwd.at[z], mid_fwd.at[z], zf_r.at[z]).start()
+    hop_fwd(3)
+    send_root(m, 0, across, (2,))
+    pass_stop(mid_fwd, stop_fwd, zf_s, stop_r.at[0], zf_r)
+    hop_fwd(4)
+    send_root(m, 0, across, (3,))
     send_root(m, 1, sibling, range(4))
-    pass_stop(mid_fwd, stop_fwd, zf_s, stop_r.at[0], zf_r)
+    hop_fwd(5)
 
     def forward_xy(qd):
         for t in range(4):
@@ -189,20 +202,19 @@
 
     total = jnp.zeros((8, LANES), F32)
     forward_xy(quads[0])
-    for step in (6, 7):
-        for sign in (1, -1):
-            send_z(send_fwd, mid_fwd, zf_s, zf_r, sign * step)
+    hop_fwd(6)
+    loads[1].wait()
+    hop_fwd(7)
     forward_xy(quads[1])
-    loads[1].wait()
     share(quads[0])
+    await_bytes(rroot.at[m_across], r_r.at[0])
+    send_root(m_across, 2, sibling, range(4))
     forward_xy(quads[2])
     share(quads[1])
+    forward_xy(quads[3])
     gather_chunk(quads[0])
     left_product(quads[0])
     total = grad_squares(quads[0], total)
-    await_bytes(rroot.at[m_across], r_r.at[0])
-    send_root(m_across, 2, sibling, range(4))
-    forward_xy(quads[3])
     share(quads[2])
     gather_chunk(quads[1])
     left_product(quads[1])
@@ -236,9 +248,8 @@
         fd = own_q * GROUP + (m + step) % GROUP
         remote(sums.at[m], sums.at[m], ex_s.at[step - 1], ex_r.at[m], z, fd).start()
     send_stop(send_back, stop_back, zb_s, stop_r.at[1])
-    for step in (1, 2, 3):
-        for sign in (1, -1):
-            send_z(send_back, mid_back, zb_s, zb_r, sign * step)
+    hop_back(1)
+    hop_back(2)
     local(send_back.at[z], mid_back.at[z], zb_r.at[z]).start()
     for step in range(1, GROUP):
         await_bytes(sums.at[0], ex_r.at[(m + step) % GROUP])
@@ -248,9 +259,8 @@
     for step in range(1, NZ):
         zd = (z + step) % NZ
         remote(gains.at[z], gains.at[z], gain_s, gain_r.at[z], zd, f).start()
-    for step in (4, 5, 6, 7):
-        for sign in (1, -1):
-            send_z(send_back, mid_back, zb_s, zb_r, sign * step)
+    hop_back(3)
+    hop_back(4)
     pass_stop(mid_back, stop_back, zb_s, stop_r.at[1], zb_r)
 
     def back_xy(qd):
@@ -301,10 +311,13 @@
     gram_left()
     stores = [local(lnew, ln_out, out_sem.at[0]), local(rnew, rn_out, out_sem.at[1])]
     stores[0].start()
+    hop_back(5)
     back_xy(quads[0])
+    hop_back(6)
     loads[4].wait()
     gram_right()
     stores[1].start()
+    hop_back(7)
     back_xy(quads[1])
     back_xy(quads[2])
     back_xy(quads[3])
@@ -312,8 +325,9 @@
     for qd in quads:
         await_bytes(final.at[:, pl.ds(qd * 4, 4)], xb_r.at[qd])
 
-    await_bytes(send_fwd, zf_s)
-    await_bytes(send_back, zb_s)
+    for sem in (zf_s, zb_s):
+        for step in (0, 6, 7):
+            await_bytes(send_fwd.at[pl.ds(0, 2)], sem.at[step])
     for c in range(4):
         await_bytes(raw.at[pl.ds(0, 15), 0, pl.ds(0, 4)], xf_s.at[c])
         await_bytes(raw.at[:, 0, pl.ds(0, 4)], sib_s.at[c])
@@ -398,13 +412,13 @@
             pltpu.VMEM((NQ, 16, LANES), BF16),
             pltpu.VMEM((NQ, 16, LANES), BF16),
             dma((5,)), dma((2,)),
-            dma, dma((NZ,)),
+            dma((8,)), dma((NZ,)),
             dma((4,)), dma((4, 4)),
             dma((4,)), dma((4,)),
             dma((3,)), dma((3,)),
             dma((3,)), dma((GROUP,)),
             dma, dma((NZ,)),
-            dma, dma((NZ,)),
+            dma((8,)), dma((NZ,)),
             dma((4,)), dma((4,)),
             dma((2,)),
         ],

time: 95.3 us -> 95.9 us (level)
  no operation moved by 1% of the time
where the time goes in v3:
time: 95.9 us; the launch traced here: 95.7 us
  Pallas kernels  95.1 us (99%)
    pallas_call x1, Pallas kernels, per_device(): pl.pallas_call(kernel, out_shape=(jax.ShapeDtypeStruct((NQ, NZ, 16, LANES...  91.5 us
    pallas_call x1, Pallas kernels, per_device(): pl.pallas_call(finish, out_shape=(jax.ShapeDtypeStruct(columns.shape, BF1...  3.57 us

profile of v3, /device:TPU:1, one launch (start us, length us, event | category | flops | bytes accessed | tf_op | source)
XLA Modules:
  0.0 95.7 jit_solution(5135205844188986227)
XLA Ops:
  0.6 91.5 %shard_map.85 = (bf16[8,16,16,128]{3,2,1,0:T(8,128)(2,1)}, bf16[256,1024]{1,0:T(8,128)(2,1)}, bf16[256,1024]{1,0:T(8,128)(2,1)}) custom-call(s32[1,128]{1,0:T(1,128)} %bitcast.7, bf16[2048,128]{1,0:T(8,128)(2,1)} %bitcast.9, bf16[256,1024]{1,0:T(8,128)(2,1)} %lf_in.1, bf16[256,1024]{1,0:T(8,128)(2,1)} %rf_in.1, bf16[256,1024]{1,0:T(8,128)(2,1)} %lr_in.1, ...), custom_call_target="tpu_custom_call" | custom-call | flops 2200000000 | bytes 8000000 | tf_op jit(solution)/shard_map/pallas_call | solution.py:388
  92.2 3.6 %shard_map.86 = (bf16[2048,128]{1,0:T(8,128)(2,1)}, bf16[256,1024]{1,0:T(8,128)(2,1)}, bf16[256,1024]{1,0:T(8,128)(2,1)}) custom-call(s32[1,128]{1,0:T(1,128)} %bitcast.8, bf16[8,16,16,128]{3,2,1,0:T(8,128)(2,1)} %get-tuple-element.9.final, bf16[256,1024]{1,0:T(8,128)(2,1)} %get-tuple-element.10.lnew, bf16[256,1024]{1,0:T(8,128)(2,1)} %get-tuple-element.11.rnew), custom_call_target="tpu_custom_call" | custom-call | flops 70000000 | bytes 4000000 | tf_op jit(solution)/shard_map/pallas_call | solution.py:430

commit v4 on v3

--- a/solution.py
+++ b/solution.py
@@ -100,22 +100,19 @@
 
     way = 1 - 2 * core
 
-    def send_z(send, mid, send_sem, recv_sem, step):
-        if step > 2:
-            await_bytes(send.at[pl.ds(0, 2)], send_sem.at[step - 2])
-        for sign in (1, -1):
-            zd = (z + sign * step * way + NZ) % NZ
-            remote(send.at[zd], mid.at[z], send_sem.at[step], recv_sem.at[z], zd, f).start()
-
-    def send_stop(send, stop, send_sem, recv_sem):
+    def by_parity(plane):
+        return plane % 2 * 8 + plane // 2
+
+    def opposite(send, stop, send_sem, recv_sem):
         zd = (z + way + NZ) % NZ
-        remote(send.at[(z + NZ // 2) % NZ], stop, send_sem.at[0], recv_sem, zd, f).start()
-
-    def pass_stop(mid, stop, send_sem, stop_sem, recv_sem):
+        remote(send.at[(z + NZ // 2) % NZ], stop, send_sem, recv_sem, zd, f).start()
+
+    def pass_stop(mid, slot, stop, send_sem, stop_sem, recv_sem):
         await_bytes(stop, stop_sem)
-        origin = (z - way + NZ) % NZ
         zd = (z + 7 * way + NZ) % NZ
-        remote(stop, mid.at[origin], send_sem.at[0], recv_sem.at[origin], zd, f).start()
+        remote(stop, mid.at[slot], send_sem, recv_sem.at[slot], zd, f).start()
+
+    behind = (z - way + NZ) % NZ
 
     def send_root(member, index, fd, parts):
         for part in parts:
@@ -123,25 +120,47 @@
             remote(rows, rows, r_s.at[index], r_r.at[index], z, fd).start()
 
     loads[2].wait()
-    def hop_fwd(step):
-        send_z(send_fwd, mid_fwd, zf_s, zf_r, step)
-
-    def hop_back(step):
-        send_z(send_back, mid_back, zb_s, zb_r, step)
-
-    send_stop(send_fwd, stop_fwd, zf_s, stop_r.at[0])
-    hop_fwd(1)
+    odd_z = z % 2
+
+    def both_fwd(step, sem):
+        for sign in (1, -1):
+            zd = (z + sign * step * way + NZ) % NZ
+            remote(send_fwd.at[zd], mid_fwd.at[z], zf_s.at[sem], zf_r.at[z], zd, f).start()
+
+    def group_fwd(phase, i):
+        sem = phase * 4 + i
+        if sem in (2, 3, 4, 6, 7):
+            await_bytes(send_fwd.at[pl.ds(0, 2)], zf_s.at[sem - 2 if sem != 4 else 2])
+        flip = odd_z if phase == 0 else 1 - odd_z
+        if i < 3:
+            both_fwd(2 * (i + 1) - flip, sem)
+            return
+
+        @pl.when(flip == 1)
+        def _():
+            both_fwd(7, sem)
+
+        @pl.when(flip == 0)
+        def _():
+            opposite(send_fwd, stop_fwd, zf_s.at[sem], stop_r.at[0])
+
+    group_fwd(0, 0)
     send_root(m, 0, across, (0,))
-    hop_fwd(2)
+    group_fwd(0, 1)
     send_root(m, 0, across, (1,))
     local(send_fwd.at[z], mid_fwd.at[z], zf_r.at[z]).start()
-    hop_fwd(3)
+    group_fwd(0, 2)
     send_root(m, 0, across, (2,))
-    pass_stop(mid_fwd, stop_fwd, zf_s, stop_r.at[0], zf_r)
-    hop_fwd(4)
+    group_fwd(0, 3)
     send_root(m, 0, across, (3,))
     send_root(m, 1, sibling, range(4))
-    hop_fwd(5)
+
+    @pl.when(odd_z == 1)
+    def _():
+        pass_stop(mid_fwd, behind, stop_fwd, zf_s.at[8], stop_r.at[0], zf_r)
+
+    group_fwd(1, 0)
+    group_fwd(1, 1)
 
     def forward_xy(qd):
         for t in range(4):
@@ -201,10 +220,15 @@
         return total + jnp.sum((rows * rows).reshape(QUARTER // 8, 8, 2, LANES), axis=(0, 2))
 
     total = jnp.zeros((8, LANES), F32)
+    group_fwd(1, 2)
+    group_fwd(1, 3)
+
+    @pl.when(odd_z == 0)
+    def _():
+        pass_stop(mid_fwd, behind, stop_fwd, zf_s.at[8], stop_r.at[0], zf_r)
+
     forward_xy(quads[0])
-    hop_fwd(6)
     loads[1].wait()
-    hop_fwd(7)
     forward_xy(quads[1])
     share(quads[0])
     await_bytes(rroot.at[m_across], r_r.at[0])
@@ -247,10 +271,19 @@
     for step in range(1, GROUP):
         fd = own_q * GROUP + (m + step) % GROUP
         remote(sums.at[m], sums.at[m], ex_s.at[step - 1], ex_r.at[m], z, fd).start()
-    send_stop(send_back, stop_back, zb_s, stop_r.at[1])
+    my_slot = by_parity(z)
+
+    def hop_back(step):
+        if step > 2:
+            await_bytes(send_back.at[pl.ds(0, 2)], zb_s.at[step - 2])
+        for sign in (1, -1):
+            zd = (z + sign * step * way + NZ) % NZ
+            remote(send_back.at[zd], mid_back.at[my_slot], zb_s.at[step], zb_r.at[my_slot], zd, f).start()
+
+    opposite(send_back, stop_back, zb_s.at[0], stop_r.at[1])
     hop_back(1)
     hop_back(2)
-    local(send_back.at[z], mid_back.at[z], zb_r.at[z]).start()
+    local(send_back.at[z], mid_back.at[my_slot], zb_r.at[my_slot]).start()
     for step in range(1, GROUP):
         await_bytes(sums.at[0], ex_r.at[(m + step) % GROUP])
     grad_sq = jnp.sum(sums[0, 0] + sums[1, 0] + sums[2, 0] + sums[3, 0], keepdims=True)
@@ -261,34 +294,35 @@
         remote(gains.at[z], gains.at[z], gain_s, gain_r.at[z], zd, f).start()
     hop_back(3)
     hop_back(4)
-    pass_stop(mid_back, stop_back, zb_s, stop_r.at[1], zb_r)
-
-    def back_xy(qd):
-        for t in range(4):
-            zs = qd * 4 + t
-            await_bytes(mid_back.at[zs], zb_r.at[zs])
-
-            @pl.when(zs != z)
+    pass_stop(mid_back, by_parity(behind), stop_back, zb_s.at[0], stop_r.at[1], zb_r)
+
+    def back_xy(chunk, start=0, count=4):
+        for t in range(count):
+            slot = chunk * 4 + start + t
+            plane = slot % 8 * 2 + slot // 8
+            await_bytes(mid_back.at[slot], zb_r.at[slot])
+
+            @pl.when(plane != z)
             def _():
-                await_bytes(gains.at[zs], gain_r.at[zs])
-
-            mid_back[zs] = (mid_back[zs].astype(F32) * gains[zs].reshape(1, 1, LANES)).astype(BF16)
+                await_bytes(gains.at[plane], gain_r.at[plane])
+
+            mid_back[slot] = (mid_back[slot].astype(F32) * gains[plane].reshape(1, 1, LANES)).astype(BF16)
         for i in range(NQ):
             d = (f % NQ + i) % NQ
             fd = m * NQ + d
-            src = mid_back.at[pl.ds(qd * 4, 4), d]
-            dst = final.at[own_q, pl.ds(qd * 4, 4)]
+            src = mid_back.at[pl.ds(chunk * 4 + start, count), d]
+            dst = final.at[own_q, pl.ds(chunk * 4 + start, count)]
             if i > 0:
-                remote(src, dst, xb_s.at[qd], xb_r.at[qd], z, fd).start()
+                remote(src, dst, xb_s.at[chunk], xb_r.at[chunk], z, fd).start()
                 continue
 
             @pl.when(x != m)
             def _():
-                remote(src, dst, xb_s.at[qd], xb_r.at[qd], z, fd).start()
+                remote(src, dst, xb_s.at[chunk], xb_r.at[chunk], z, fd).start()
 
             @pl.when(x == m)
             def _():
-                local(src, dst, xb_r.at[qd]).start()
+                local(src, dst, xb_r.at[chunk]).start()
 
     def gram_left():
         rows = pl.ds(pl.multiple_of(m * QUARTER, QUARTER), QUARTER)
@@ -312,22 +346,32 @@
     stores = [local(lnew, ln_out, out_sem.at[0]), local(rnew, rn_out, out_sem.at[1])]
     stores[0].start()
     hop_back(5)
-    back_xy(quads[0])
     hop_back(6)
     loads[4].wait()
     gram_right()
     stores[1].start()
     hop_back(7)
-    back_xy(quads[1])
-    back_xy(quads[2])
-    back_xy(quads[3])
-
-    for qd in quads:
-        await_bytes(final.at[:, pl.ds(qd * 4, 4)], xb_r.at[qd])
-
-    for sem in (zf_s, zb_s):
-        for step in (0, 6, 7):
-            await_bytes(send_fwd.at[pl.ds(0, 2)], sem.at[step])
+    half = z // 8
+    back_xy(half)
+    back_xy(1 - half)
+    back_xy(2 + half)
+    back_xy(3 - half, 0, 2)
+    back_xy(3 - half, 2, 2)
+
+    for chunk in range(4):
+        await_bytes(final.at[:, pl.ds(chunk * 4, 4)], xb_r.at[chunk])
+
+    await_bytes(stop_fwd, zf_s.at[8])
+    for sem, paired in ((3, odd_z == 1), (7, odd_z == 0)):
+        await_bytes(stop_fwd, zf_s.at[sem])
+
+        @pl.when(paired)
+        def _():
+            await_bytes(stop_fwd, zf_s.at[sem])
+
+    await_bytes(send_fwd.at[pl.ds(0, 2)], zf_s.at[6])
+    for step in (0, 6, 7):
+        await_bytes(send_back.at[pl.ds(0, 2)], zb_s.at[step])
     for c in range(4):
         await_bytes(raw.at[pl.ds(0, 15), 0, pl.ds(0, 4)], xf_s.at[c])
         await_bytes(raw.at[:, 0, pl.ds(0, 4)], sib_s.at[c])
@@ -360,7 +404,9 @@
     for copy in loads:
         copy.start()
     row = lax.broadcasted_iota(jnp.int32, (LANES, LANES), 0)
-    slot_of = (row % NZ) * NQ + row // NZ
+    place_of = lax.rem(row, NZ)
+    plane = lax.rem(place_of, NZ // 2) * 2 + lax.div(place_of, NZ // 2)
+    slot_of = plane * NQ + lax.div(row, NZ)
     place = (jnp.broadcast_to(owner_ref[...], (LANES, LANES)) == slot_of).astype(BF16)
     for q in range(NQ):
         loads[q].wait()
@@ -412,7 +458,7 @@
             pltpu.VMEM((NQ, 16, LANES), BF16),
             pltpu.VMEM((NQ, 16, LANES), BF16),
             dma((5,)), dma((2,)),
-            dma((8,)), dma((NZ,)),
+            dma((9,)), dma((NZ,)),
             dma((4,)), dma((4, 4)),
             dma((4,)), dma((4,)),
             dma((3,)), dma((3,)),

time: 95.9 us -> 102 us (1.064)
  Pallas kernels: 95.1 us -> 101 us
    pallas_call x1, Pallas kernels: 91.5 us -> 97.3 us  [per_device(): pl.pallas_call(kernel, out_shape=(jax.ShapeDtypeStruct((NQ, NZ, 16, LANES...]
where the time goes in v4:
time: 102 us
  Pallas kernels  101 us (99%)
    pallas_call x1, Pallas kernels, per_device(): pl.pallas_call(kernel, out_shape=(jax.ShapeDtypeStruct((NQ, NZ, 16, LANES...  97.3 us
    pallas_call x1, Pallas kernels, per_device(): pl.pallas_call(finish, out_shape=(jax.ShapeDtypeStruct(columns.shape, BF1...  3.57 us

profile of v4, /device:TPU:1, one launch (start us, length us, event | category | flops | bytes accessed | tf_op | source)
XLA Modules:
  0.0 101.5 jit_solution(7214190709048374890)
XLA Ops:
  0.6 97.3 %shard_map.85 = (bf16[8,16,16,128]{3,2,1,0:T(8,128)(2,1)}, bf16[256,1024]{1,0:T(8,128)(2,1)}, bf16[256,1024]{1,0:T(8,128)(2,1)}) custom-call(s32[1,128]{1,0:T(1,128)} %bitcast.7, bf16[2048,128]{1,0:T(8,128)(2,1)} %bitcast.9, bf16[256,1024]{1,0:T(8,128)(2,1)} %lf_in.1, bf16[256,1024]{1,0:T(8,128)(2,1)} %rf_in.1, bf16[256,1024]{1,0:T(8,128)(2,1)} %lr_in.1, ...), custom_call_target="tpu_custom_call" | custom-call | flops 2200000000 | bytes 8000000 | tf_op jit(solution)/shard_map/pallas_call | solution.py:434
  98.0 3.6 %shard_map.86 = (bf16[2048,128]{1,0:T(8,128)(2,1)}, bf16[256,1024]{1,0:T(8,128)(2,1)}, bf16[256,1024]{1,0:T(8,128)(2,1)}) custom-call(s32[1,128]{1,0:T(1,128)} %bitcast.8, bf16[8,16,16,128]{3,2,1,0:T(8,128)(2,1)} %get-tuple-element.9.final, bf16[256,1024]{1,0:T(8,128)(2,1)} %get-tuple-element.10.lnew, bf16[256,1024]{1,0:T(8,128)(2,1)} %get-tuple-element.11.rnew), custom_call_target="tpu_custom_call" | custom-call | flops 70000000 | bytes 4000000 | tf_op jit(solution)/shard_map/pallas_call | solution.py:476

commit v5 on v2

--- a/solution.py
+++ b/solution.py
@@ -66,8 +66,8 @@
 
     loads = [
         local(grad_in, grad, in_sem.at[0]),
-        local(lr_in, lroot, in_sem.at[1]),
-        local(rr_in, rroot.at[m], in_sem.at[2]),
+        local(lr_in, lroot.at[core], in_sem.at[1]),
+        local(rr_in, rroot.at[0], in_sem.at[2]),
         local(lf_in, lfac, in_sem.at[3]),
         local(rf_in, rfac, in_sem.at[4]),
     ]
@@ -83,8 +83,13 @@
         pl.semaphore_signal(barrier, inc=1, device_id=((z + i) % NZ, f), device_id_type=MESH)
         return carry
 
+    def greet_senders(i, carry):
+        pl.semaphore_signal(barrier, inc=1, device_id=((z + i) % NZ, sibling), device_id_type=MESH)
+        return carry
+
     lax.fori_loop(1, NZ, greet_ring, 0)
     lax.fori_loop(1, NF, greet_plane, 0)
+    lax.fori_loop(1, NZ, greet_senders, 0)
 
     owner = owner_ref[...]
     slot_row = lax.broadcasted_iota(jnp.int32, (LANES, LANES), 0)
@@ -96,7 +101,7 @@
     for zd in range(NZ):
         send_fwd[zd] = wide[zd * 128 : zd * 128 + 128, :].reshape(NQ, 16, LANES).astype(BF16)
 
-    pl.semaphore_wait(barrier, NZ - 1 + NF - 1)
+    pl.semaphore_wait(barrier, 2 * (NZ - 1) + NF - 1)
 
     way = 1 - 2 * core
 
@@ -114,20 +119,24 @@
         zd = (z + 7 * way + NZ) % NZ
         remote(stop, mid.at[origin], send_sem, recv_sem.at[origin], zd, f).start()
 
-    def send_root(member, index, fd, parts):
-        for part in parts:
-            rows = rroot.at[member, pl.ds(part * 64, 64)]
-            remote(rows, rows, r_s.at[index], r_r.at[index], z, fd).start()
-
+    def send_right(part):
+        rows = pl.ds(part * 64, 64)
+        remote(rroot.at[0, rows], rroot.at[1, rows], r_s.at[0], r_r.at[0], z, across).start()
+
+    def send_left(part):
+        rows = lroot.at[core, pl.ds(part * 64, 64)]
+        remote(rows, rows, r_s.at[1], r_r.at[1], z, sibling).start()
+
+    loads[1].wait()
     loads[2].wait()
     send_stop(send_fwd, stop_fwd, zf_s, stop_r.at[0])
     for step in range(1, 6):
         for sign in (1, -1):
             send_z(send_fwd, mid_fwd, zf_s, zf_r, sign * step)
         if step < 5:
-            send_root(m, 0, across, (step - 1,))
+            send_right(step - 1)
+            send_left(step - 1)
     local(send_fwd.at[z], mid_fwd.at[z], zf_r.at[z]).start()
-    send_root(m, 1, sibling, range(4))
     pass_stop(mid_fwd, stop_fwd, zf_s, stop_r.at[0], zf_r)
 
     def forward_xy(qd):
@@ -168,20 +177,22 @@
         lax.fori_loop(0, NF // 4, unpack, 0)
 
     def left_product(qd):
-        tpart[qd] = jnp.dot(lroot[...], block[qd], preferred_element_type=F32).astype(BF16)
-
-    def right_part(qd, j):
+        for k in range(2):
+            tpart[k, qd] = jnp.dot(lroot[k], block[qd], preferred_element_type=F32).astype(BF16)
+
+    def right_part(qd, k, j):
         return lax.dot_general(
-            tpart[qd], rroot[j, :, pl.ds(pl.multiple_of(qd * QUARTER, QUARTER), QUARTER)], NT,
+            tpart[k, qd], rroot[j, :, pl.ds(pl.multiple_of(qd * QUARTER, QUARTER), QUARTER)], NT,
             preferred_element_type=F32,
         )
 
     def right_product(qd, first=False):
-        for j in range(GROUP):
-            if first:
-                acc[j] = right_part(qd, j)
-            else:
-                acc[j] += right_part(qd, j)
+        for k in range(2):
+            for j in range(2):
+                if first:
+                    acc[2 * k + j] = right_part(qd, k, j)
+                else:
+                    acc[2 * k + j] += right_part(qd, k, j)
 
     def grad_squares(qd, total):
         rows = block[qd, pl.ds(pl.multiple_of(m * QUARTER, QUARTER), QUARTER), :].astype(F32)
@@ -193,22 +204,19 @@
         for sign in (1, -1):
             send_z(send_fwd, mid_fwd, zf_s, zf_r, sign * step)
     forward_xy(quads[1])
-    loads[1].wait()
     share(quads[0])
     forward_xy(quads[2])
     share(quads[1])
     gather_chunk(quads[0])
+    await_bytes(lroot.at[0], r_r.at[1])
     left_product(quads[0])
     total = grad_squares(quads[0], total)
-    await_bytes(rroot.at[m_across], r_r.at[0])
-    send_root(m_across, 2, sibling, range(4))
     forward_xy(quads[3])
     share(quads[2])
     gather_chunk(quads[1])
     left_product(quads[1])
     total = grad_squares(quads[1], total)
-    await_bytes(rroot.at[0], r_r.at[1])
-    await_bytes(rroot.at[0], r_r.at[2])
+    await_bytes(rroot.at[1], r_r.at[0])
     right_product(quads[0], first=True)
     right_product(quads[1])
     share(quads[3])
@@ -220,26 +228,50 @@
     left_product(quads[3])
 
     prec_total = jnp.zeros((8, LANES), F32)
-    for c in range(4):
-        value = (acc[c] + right_part(quads[3], c)).astype(BF16)
-        for pair in range(2):
-            rows = value[:, pair * LANES : (pair + 1) * LANES].reshape(NQ, 2, 16, LANES)
-            even, odd = halves(rows[:, 0].reshape(LANES, LANES), rows[:, 1].reshape(LANES, LANES))
-            send_back[c * 4 + 2 * pair] = even.reshape(NQ, 16, LANES)
-            send_back[c * 4 + 2 * pair + 1] = odd.reshape(NQ, 16, LANES)
-        wider = value.astype(F32)
-        prec_total += jnp.sum((wider * wider).reshape(QUARTER // 8, 8, 2, LANES), axis=(0, 2))
+    for k in range(2):
+        for j in range(2):
+            value = (acc[2 * k + j] + right_part(quads[3], k, j)).astype(BF16)
+            for pair in range(2):
+                rows = value[:, pair * LANES : (pair + 1) * LANES].reshape(NQ, 2, 16, LANES)
+                even, odd = halves(rows[:, 0].reshape(LANES, LANES), rows[:, 1].reshape(LANES, LANES))
+                send_back[k, j, 2 * pair] = even.reshape(NQ, 16, LANES)
+                send_back[k, j, 2 * pair + 1] = odd.reshape(NQ, 16, LANES)
+            wider = value.astype(F32)
+            prec_total += jnp.sum((wider * wider).reshape(QUARTER // 8, 8, 2, LANES), axis=(0, 2))
 
     sums[m, 0] = grad_squares(quads[3], total)
     sums[m, 1] = prec_total
     for step in range(1, GROUP):
         fd = own_q * GROUP + (m + step) % GROUP
         remote(sums.at[m], sums.at[m], ex_s.at[step - 1], ex_r.at[m], z, fd).start()
-    send_stop(send_back, stop_back, zb_s, stop_r.at[1])
-    for step in (1, 2, 3):
-        for sign in (1, -1):
-            send_z(send_back, mid_back, zb_s, zb_r, sign * step)
-    local(send_back.at[z], mid_back.at[z], zb_r.at[z]).start()
+    def send_rows(k, j, t):
+        piece = send_back.at[k, j, t]
+        zd = (m if j == 0 else m_across) * 4 + t
+        fd = f - core + k
+        here = zd == z
+
+        @pl.when(here & (core == k))
+        def _():
+            local(piece, mid_back.at[z], zb_r.at[z]).start()
+
+        @pl.when(here & (core != k))
+        def _():
+            remote(piece, mid_back.at[z], zb_s, zb_r.at[z], z, sibling).start()
+
+        far = zd == (z + NZ // 2) % NZ
+
+        @pl.when(far)
+        def _():
+            remote(piece, stop_back, zb_s, stop_r.at[1], (z + NZ + 1 - 2 * k) % NZ, fd).start()
+
+        @pl.when(jnp.logical_not(here | far))
+        def _():
+            remote(piece, mid_back.at[z], zb_s, zb_r.at[z], zd, fd).start()
+
+    for t in range(2):
+        for j in range(2):
+            for k in range(2):
+                send_rows(k, j, t)
     for step in range(1, GROUP):
         await_bytes(sums.at[0], ex_r.at[(m + step) % GROUP])
     grad_sq = jnp.sum(sums[0, 0] + sums[1, 0] + sums[2, 0] + sums[3, 0], keepdims=True)
@@ -248,9 +280,10 @@
     for step in range(1, NZ):
         zd = (z + step) % NZ
         remote(gains.at[z], gains.at[z], gain_s, gain_r.at[z], zd, f).start()
-    for step in (4, 5, 6, 7):
-        for sign in (1, -1):
-            send_z(send_back, mid_back, zb_s, zb_r, sign * step)
+    for t in range(2, 4):
+        for j in range(2):
+            for k in range(2):
+                send_rows(k, j, t)
     pass_stop(mid_back, stop_back, zb_s, stop_r.at[1], zb_r)
 
     def back_xy(qd):
@@ -313,7 +346,12 @@
         await_bytes(final.at[:, pl.ds(qd * 4, 4)], xb_r.at[qd])
 
     await_bytes(send_fwd, zf_s)
-    await_bytes(send_back, zb_s)
+    await_bytes(send_fwd, zb_s)
+
+    @pl.when(zq % 2 != core)
+    def _():
+        await_bytes(stop_back, zb_s)
+
     for c in range(4):
         await_bytes(raw.at[pl.ds(0, 15), 0, pl.ds(0, 4)], xf_s.at[c])
         await_bytes(raw.at[:, 0, pl.ds(0, 4)], sib_s.at[c])
@@ -327,8 +365,9 @@
             await_bytes(final.at[:, pl.ds(0, 4)], xb_s.at[c])
 
     await_bytes(gains.at[pl.ds(0, NZ - 1)], gain_s)
+    for i in range(2):
+        await_bytes(rroot.at[0], r_s.at[i])
     for i in range(3):
-        await_bytes(rroot.at[0], r_s.at[i])
         await_bytes(sums.at[0], ex_s.at[i])
     stores[0].wait()
     stores[1].wait()
@@ -383,15 +422,15 @@
             pltpu.VMEM((NZ, NQ, 16, LANES), BF16),
             pltpu.VMEM((NF // 2, 2, NZ, 16, LANES), BF16),
             pltpu.VMEM((4, B, QUARTER), BF16),
-            pltpu.VMEM((QUARTER, B), BF16),
-            pltpu.VMEM((GROUP, QUARTER, B), BF16),
-            pltpu.VMEM((QUARTER, B), BF16),
-            pltpu.VMEM((QUARTER, B), BF16),
-            pltpu.VMEM((4, QUARTER, QUARTER), BF16),
+            pltpu.VMEM((2, QUARTER, B), BF16),
+            pltpu.VMEM((2, QUARTER, B), BF16),
+            pltpu.VMEM((QUARTER, B), BF16),
+            pltpu.VMEM((QUARTER, B), BF16),
+            pltpu.VMEM((2, 4, QUARTER, QUARTER), BF16),
             pltpu.VMEM((GROUP, QUARTER, QUARTER), F32),
             pltpu.VMEM((NZ, 1, LANES), F32),
             pltpu.VMEM((GROUP, 2, 8, LANES), F32),
-            pltpu.VMEM((NZ, NQ, 16, LANES), BF16),
+            pltpu.VMEM((2, 2, 4, NQ, 16, LANES), BF16),
             pltpu.VMEM((NZ, NQ, 16, LANES), BF16),
             pltpu.VMEM((QUARTER, B), BF16),
             pltpu.VMEM((QUARTER, B), BF16),
@@ -401,7 +440,7 @@
             dma, dma((NZ,)),
             dma((4,)), dma((4, 4)),
             dma((4,)), dma((4,)),
-            dma((3,)), dma((3,)),
+            dma((2,)), dma((2,)),
             dma((3,)), dma((GROUP,)),
             dma, dma((NZ,)),
             dma, dma((NZ,)),

time: 95.3 us -> 95.8 us (level)
  no operation moved by 1% of the time
where the time goes in v5:
time: 95.8 us; the launch traced here: 95.6 us
  Pallas kernels  95 us (99%)
    pallas_call x1, Pallas kernels, per_device(): pl.pallas_call(kernel, out_shape=(jax.ShapeDtypeStruct((NQ, NZ, 16, LANES...  91.4 us
    pallas_call x1, Pallas kernels, per_device(): pl.pallas_call(finish, out_shape=(jax.ShapeDtypeStruct(columns.shape, BF1...  3.57 us

profile of v5, /device:TPU:1, one launch (start us, length us, event | category | flops | bytes accessed | tf_op | source)
XLA Modules:
  0.0 95.6 jit_solution(1301024208595574229)
XLA Ops:
  0.6 91.4 %shard_map.85 = (bf16[8,16,16,128]{3,2,1,0:T(8,128)(2,1)}, bf16[256,1024]{1,0:T(8,128)(2,1)}, bf16[256,1024]{1,0:T(8,128)(2,1)}) custom-call(s32[1,128]{1,0:T(1,128)} %bitcast.7, bf16[2048,128]{1,0:T(8,128)(2,1)} %bitcast.9, bf16[256,1024]{1,0:T(8,128)(2,1)} %lf_in.1, bf16[256,1024]{1,0:T(8,128)(2,1)} %rf_in.1, bf16[256,1024]{1,0:T(8,128)(2,1)} %lr_in.1, ...), custom_call_target="tpu_custom_call" | custom-call | flops 2200000000 | bytes 8000000 | tf_op jit(solution)/shard_map/pallas_call | solution.py:413
  92.1 3.6 %shard_map.86 = (bf16[2048,128]{1,0:T(8,128)(2,1)}, bf16[256,1024]{1,0:T(8,128)(2,1)}, bf16[256,1024]{1,0:T(8,128)(2,1)}) custom-call(s32[1,128]{1,0:T(1,128)} %bitcast.8, bf16[8,16,16,128]{3,2,1,0:T(8,128)(2,1)} %get-tuple-element.9.final, bf16[256,1024]{1,0:T(8,128)(2,1)} %get-tuple-element.10.lnew, bf16[256,1024]{1,0:T(8,128)(2,1)} %get-tuple-element.11.rnew), custom_call_target="tpu_custom_call" | custom-call | flops 70000000 | bytes 4000000 | tf_op jit(solution)/shard_map/pallas_call | solution.py:455

commit v6 on v2

--- a/solution.py
+++ b/solution.py
@@ -49,6 +49,7 @@
     sibling = f + 1 - 2 * core
     across = f + 2 - 4 * (m // 2)
     m_across = m + 2 - 4 * (m // 2)
+    early = 2 * (1 - (z % 4) // 2)
     near = 1 + 2 * (1 - (z % 4) // 2)
     quads = [zq, (zq + near) % 4, (zq + 4 - near) % 4, (zq + 2) % 4]
 
@@ -90,9 +91,12 @@
     slot_row = lax.broadcasted_iota(jnp.int32, (LANES, LANES), 0)
     pick = (jnp.broadcast_to(owner, (LANES, LANES)) == slot_row).astype(BF16)
     loads[0].wait()
-    for t in range(16):
-        piece = jnp.concatenate((grad[t * 64 : t * 64 + 64, :], grad[(16 + t) * 64 : (16 + t) * 64 + 64, :]), axis=0)
-        wide[pl.ds(t, LANES, stride=16), :] = lax.dot_general(pick, piece, NT, preferred_element_type=F32)
+    for t in range(0, 16, 2):
+        starts = (t, 16 + t, t + 1, 17 + t)
+        piece = jnp.concatenate([grad[r * 64 : r * 64 + 64, :] for r in starts], axis=0)
+        tiles = lax.dot_general(pick, piece, NT, preferred_element_type=F32)
+        wide[pl.ds(t, LANES, stride=16), :] = tiles[:, :LANES]
+        wide[pl.ds(t + 1, LANES, stride=16), :] = tiles[:, LANES:]
     for zd in range(NZ):
         send_fwd[zd] = wide[zd * 128 : zd * 128 + 128, :].reshape(NQ, 16, LANES).astype(BF16)
 
@@ -130,15 +134,17 @@
     send_root(m, 1, sibling, range(4))
     pass_stop(mid_fwd, stop_fwd, zf_s, stop_r.at[0], zf_r)
 
-    def forward_xy(qd):
-        for t in range(4):
-            await_bytes(mid_fwd.at[qd * 4 + t], zf_r.at[qd * 4 + t])
+    def forward_xy(qd, start=0, count=4):
+        for t in range(count):
+            zs = qd * 4 + start + t
+            await_bytes(mid_fwd.at[zs], zf_r.at[zs])
+        sources = pl.ds(qd * 4 + start, count)
 
         for i in range(NF // 2):
             chip = (xy + i) % (NF // 2)
             q = chip // 2
-            src = mid_fwd.at[pl.ds(qd * 4, 4), q]
-            dst = raw.at[xy, core, pl.ds(qd * 4, 4)]
+            src = mid_fwd.at[sources, q]
+            dst = raw.at[xy, core, sources]
             if i == 0:
                 local(src, dst, xf_r.at[qd, x]).start()
             else:
@@ -157,15 +163,15 @@
         def unpack(i, carry):
             for pair in range(2):
                 first = qd * 4 + 2 * pair
-                even = raw[pl.ds(i * 2, 2), :, first].reshape(64, LANES)
-                odd = raw[pl.ds(i * 2, 2), :, first + 1].reshape(64, LANES)
+                even = raw[pl.ds(i * 4, 4), :, first].reshape(128, LANES)
+                odd = raw[pl.ds(i * 4, 4), :, first + 1].reshape(128, LANES)
                 top, bottom = halves(even, odd)
-                rows = jnp.concatenate((top.reshape(4, 16, LANES), bottom.reshape(4, 16, LANES)), axis=1)
-                at = pl.multiple_of(i * 128, 128)
-                block[qd, pl.ds(at, 128), pair * LANES : (pair + 1) * LANES] = rows.reshape(128, LANES)
+                rows = jnp.concatenate((top.reshape(8, 16, LANES), bottom.reshape(8, 16, LANES)), axis=1)
+                at = pl.multiple_of(i * 256, 256)
+                block[qd, pl.ds(at, 256), pair * LANES : (pair + 1) * LANES] = rows.reshape(256, LANES)
             return carry
 
-        lax.fori_loop(0, NF // 4, unpack, 0)
+        lax.fori_loop(0, NF // 8, unpack, 0)
 
     def left_product(qd):
         tpart[qd] = jnp.dot(lroot[...], block[qd], preferred_element_type=F32).astype(BF16)
@@ -197,12 +203,13 @@
     share(quads[0])
     forward_xy(quads[2])
     share(quads[1])
+    forward_xy(quads[3], early, 2)
     gather_chunk(quads[0])
     left_product(quads[0])
     total = grad_squares(quads[0], total)
     await_bytes(rroot.at[m_across], r_r.at[0])
     send_root(m_across, 2, sibling, range(4))
-    forward_xy(quads[3])
+    forward_xy(quads[3], 2 - early, 2)
     share(quads[2])
     gather_chunk(quads[1])
     left_product(quads[1])
@@ -219,16 +226,35 @@
     gather_chunk(quads[3])
     left_product(quads[3])
 
-    prec_total = jnp.zeros((8, LANES), F32)
-    for c in range(4):
-        value = (acc[c] + right_part(quads[3], c)).astype(BF16)
+    def last_product(qd):
+        value = (acc[qd] + right_part(quads[3], qd)).astype(BF16)
         for pair in range(2):
             rows = value[:, pair * LANES : (pair + 1) * LANES].reshape(NQ, 2, 16, LANES)
             even, odd = halves(rows[:, 0].reshape(LANES, LANES), rows[:, 1].reshape(LANES, LANES))
-            send_back[c * 4 + 2 * pair] = even.reshape(NQ, 16, LANES)
-            send_back[c * 4 + 2 * pair + 1] = odd.reshape(NQ, 16, LANES)
+            send_back[qd * 4 + 2 * pair] = even.reshape(NQ, 16, LANES)
+            send_back[qd * 4 + 2 * pair + 1] = odd.reshape(NQ, 16, LANES)
         wider = value.astype(F32)
-        prec_total += jnp.sum((wider * wider).reshape(QUARTER // 8, 8, 2, LANES), axis=(0, 2))
+        return jnp.sum((wider * wider).reshape(QUARTER // 8, 8, 2, LANES), axis=(0, 2))
+
+    def send_quad(qd, skip=None):
+        for t in range(4):
+            zd = qd * 4 + t
+
+            def start():
+                remote(send_back.at[zd], mid_back.at[z], zb_s, zb_r.at[z], zd, f).start()
+
+            if skip is None:
+                start()
+            else:
+                pl.when(zd != skip)(start)
+
+    prec_total = last_product(quads[0])
+    send_quad(quads[0], skip=z)
+    local(send_back.at[z], mid_back.at[z], zb_r.at[z]).start()
+    prec_total += last_product(quads[1])
+    send_quad(quads[1])
+    prec_total += last_product(quads[2])
+    prec_total += last_product(quads[3])
 
     sums[m, 0] = grad_squares(quads[3], total)
     sums[m, 1] = prec_total
@@ -236,10 +262,7 @@
         fd = own_q * GROUP + (m + step) % GROUP
         remote(sums.at[m], sums.at[m], ex_s.at[step - 1], ex_r.at[m], z, fd).start()
     send_stop(send_back, stop_back, zb_s, stop_r.at[1])
-    for step in (1, 2, 3):
-        for sign in (1, -1):
-            send_z(send_back, mid_back, zb_s, zb_r, sign * step)
-    local(send_back.at[z], mid_back.at[z], zb_r.at[z]).start()
+    send_quad(quads[2])
     for step in range(1, GROUP):
         await_bytes(sums.at[0], ex_r.at[(m + step) % GROUP])
     grad_sq = jnp.sum(sums[0, 0] + sums[1, 0] + sums[2, 0] + sums[3, 0], keepdims=True)
@@ -248,14 +271,12 @@
     for step in range(1, NZ):
         zd = (z + step) % NZ
         remote(gains.at[z], gains.at[z], gain_s, gain_r.at[z], zd, f).start()
-    for step in (4, 5, 6, 7):
-        for sign in (1, -1):
-            send_z(send_back, mid_back, zb_s, zb_r, sign * step)
+    send_quad(quads[3], skip=(z + NZ // 2) % NZ)
     pass_stop(mid_back, stop_back, zb_s, stop_r.at[1], zb_r)
 
-    def back_xy(qd):
-        for t in range(4):
-            zs = qd * 4 + t
+    def back_xy(qd, start=0, count=4):
+        for t in range(count):
+            zs = qd * 4 + start + t
             await_bytes(mid_back.at[zs], zb_r.at[zs])
 
             @pl.when(zs != z)
@@ -266,8 +287,8 @@
         for i in range(NQ):
             d = (f % NQ + i) % NQ
             fd = m * NQ + d
-            src = mid_back.at[pl.ds(qd * 4, 4), d]
-            dst = final.at[own_q, pl.ds(qd * 4, 4)]
+            src = mid_back.at[pl.ds(qd * 4 + start, count), d]
+            dst = final.at[own_q, pl.ds(qd * 4 + start, count)]
             if i > 0:
                 remote(src, dst, xb_s.at[qd], xb_r.at[qd], z, fd).start()
                 continue
@@ -307,7 +328,8 @@
     stores[1].start()
     back_xy(quads[1])
     back_xy(quads[2])
-    back_xy(quads[3])
+    back_xy(quads[3], early, 2)
+    back_xy(quads[3], 2 - early, 2)
 
     for qd in quads:
         await_bytes(final.at[:, pl.ds(qd * 4, 4)], xb_r.at[qd])
@@ -339,8 +361,10 @@
     stores = [
         pltpu.make_async_copy(lvmem, ln_out, out_sem.at[0]),
         pltpu.make_async_copy(rvmem, rn_out, out_sem.at[1]),
-        pltpu.make_async_copy(dirv, dir_out, out_sem.at[2]),
     ]
+    for i, at in enumerate((0, 1024, 512, 1536)):
+        rows = pl.ds(at, 512)
+        stores.append(pltpu.make_async_copy(dirv.at[rows], dir_out.at[rows], out_sem.at[2 + i]))
     loads.append(pltpu.make_async_copy(lnew, lvmem, in_sem.at[NQ]))
     loads.append(pltpu.make_async_copy(rnew, rvmem, in_sem.at[NQ + 1]))
     for copy in loads:
@@ -359,7 +383,11 @@
         blocks = lax.dot_general(rows, place, TN, preferred_element_type=F32).astype(BF16)
         dirv[t * 64 : t * 64 + 64, :] = blocks[:64]
         dirv[(16 + t) * 64 : (16 + t) * 64 + 64, :] = blocks[64:]
-    stores[2].start()
+        if t == 7:
+            stores[2].start()
+            stores[3].start()
+    stores[4].start()
+    stores[5].start()
     for copy in stores:
         copy.wait()
 
@@ -425,7 +453,7 @@
             pltpu.VMEM((QUARTER, B), BF16),
             pltpu.VMEM((QUARTER, B), BF16),
             dma((NQ + 2,)),
-            dma((3,)),
+            dma((6,)),
         ],
         compiler_params=pltpu.CompilerParams(vmem_limit_bytes=60 * 1024 * 1024),
         cost_estimate=pl.CostEstimate(flops=70_000_000, bytes_accessed=4_000_000, transcendentals=0),

time: 95.3 us -> 98.2 us (1.030)
  Pallas kernels: 94.5 us -> 97.3 us
    pallas_call x1, Pallas kernels: 90.9 us -> 93.8 us  [per_device(): pl.pallas_call(kernel, out_shape=(jax.ShapeDtypeStruct((NQ, NZ, 16, LANES...]
where the time goes in v6:
time: 98.2 us; the launch traced here: 98 us
  Pallas kernels  97.3 us (99%)
    pallas_call x1, Pallas kernels, per_device(): pl.pallas_call(kernel, out_shape=(jax.ShapeDtypeStruct((NQ, NZ, 16, LANES...  93.8 us
    pallas_call x1, Pallas kernels, per_device(): pl.pallas_call(finish, out_shape=(jax.ShapeDtypeStruct(columns.shape, BF1...  3.5 us

profile of v6, /device:TPU:1, one launch (start us, length us, event | category | flops | bytes accessed | tf_op | source)
XLA Modules:
  0.0 98.0 jit_solution(3727747008213172106)
XLA Ops:
  0.6 93.8 %shard_map.85 = (bf16[8,16,16,128]{3,2,1,0:T(8,128)(2,1)}, bf16[256,1024]{1,0:T(8,128)(2,1)}, bf16[256,1024]{1,0:T(8,128)(2,1)}) custom-call(s32[1,128]{1,0:T(1,128)} %bitcast.7, bf16[2048,128]{1,0:T(8,128)(2,1)} %bitcast.9, bf16[256,1024]{1,0:T(8,128)(2,1)} %lf_in.1, bf16[256,1024]{1,0:T(8,128)(2,1)} %rf_in.1, bf16[256,1024]{1,0:T(8,128)(2,1)} %lr_in.1, ...), custom_call_target="tpu_custom_call" | custom-call | flops 2200000000 | bytes 8000000 | tf_op jit(solution)/shard_map/pallas_call | solution.py:402
  94.5 3.5 %shard_map.86 = (bf16[2048,128]{1,0:T(8,128)(2,1)}, bf16[256,1024]{1,0:T(8,128)(2,1)}, bf16[256,1024]{1,0:T(8,128)(2,1)}) custom-call(s32[1,128]{1,0:T(1,128)} %bitcast.8, bf16[8,16,16,128]{3,2,1,0:T(8,128)(2,1)} %get-tuple-element.9.final, bf16[256,1024]{1,0:T(8,128)(2,1)} %get-tuple-element.10.lnew, bf16[256,1024]{1,0:T(8,128)(2,1)} %get-tuple-element.11.rnew), custom_call_target="tpu_custom_call" | custom-call | flops 70000000 | bytes 4000000 | tf_op jit(solution)/shard_map/pallas_call | solution.py:444

commit v7 on v2

--- a/solution.py
+++ b/solution.py
@@ -21,6 +21,10 @@
 LANES = 128
 NT = (((1,), (1,)), ((), ()))
 TN = (((0,), (0,)), ((), ()))
+def in_turn(count):
+    return [0] + [sign * i for i in range(1, count // 2) for sign in (1, -1)] + [count // 2]
+
+
 def halves(even, odd):
     lane = lax.broadcasted_iota(jnp.int32, even.shape, even.ndim - 1)
     low = lane < LANES // 2
@@ -134,8 +138,8 @@
         for t in range(4):
             await_bytes(mid_fwd.at[qd * 4 + t], zf_r.at[qd * 4 + t])
 
-        for i in range(NF // 2):
-            chip = (xy + i) % (NF // 2)
+        for i in in_turn(NF // 2):
+            chip = (xy + i * way + NF // 2) % (NF // 2)
             q = chip // 2
             src = mid_fwd.at[pl.ds(qd * 4, 4), q]
             dst = raw.at[xy, core, pl.ds(qd * 4, 4)]
@@ -263,12 +267,12 @@
                 await_bytes(gains.at[zs], gain_r.at[zs])
 
             mid_back[zs] = (mid_back[zs].astype(F32) * gains[zs].reshape(1, 1, LANES)).astype(BF16)
-        for i in range(NQ):
-            d = (f % NQ + i) % NQ
+        for i in in_turn(NQ):
+            d = (f % NQ + i * way + NQ) % NQ
             fd = m * NQ + d
             src = mid_back.at[pl.ds(qd * 4, 4), d]
             dst = final.at[own_q, pl.ds(qd * 4, 4)]
-            if i > 0:
+            if i != 0:
                 remote(src, dst, xb_s.at[qd], xb_r.at[qd], z, fd).start()
                 continue
 
@@ -339,8 +343,10 @@
     stores = [
         pltpu.make_async_copy(lvmem, ln_out, out_sem.at[0]),
         pltpu.make_async_copy(rvmem, rn_out, out_sem.at[1]),
-        pltpu.make_async_copy(dirv, dir_out, out_sem.at[2]),
     ]
+    for i, at in enumerate((0, 1024, 512, 1536)):
+        rows = pl.ds(at, 512)
+        stores.append(pltpu.make_async_copy(dirv.at[rows], dir_out.at[rows], out_sem.at[2 + i]))
     loads.append(pltpu.make_async_copy(lnew, lvmem, in_sem.at[NQ]))
     loads.append(pltpu.make_async_copy(rnew, rvmem, in_sem.at[NQ + 1]))
     for copy in loads:
@@ -359,7 +365,11 @@
         blocks = lax.dot_general(rows, place, TN, preferred_element_type=F32).astype(BF16)
         dirv[t * 64 : t * 64 + 64, :] = blocks[:64]
         dirv[(16 + t) * 64 : (16 + t) * 64 + 64, :] = blocks[64:]
-    stores[2].start()
+        if t == 7:
+            stores[2].start()
+            stores[3].start()
+    stores[4].start()
+    stores[5].start()
     for copy in stores:
         copy.wait()
 
@@ -425,7 +435,7 @@
             pltpu.VMEM((QUARTER, B), BF16),
             pltpu.VMEM((QUARTER, B), BF16),
             dma((NQ + 2,)),
-            dma((3,)),
+            dma((6,)),
         ],
         compiler_params=pltpu.CompilerParams(vmem_limit_bytes=60 * 1024 * 1024),
         cost_estimate=pl.CostEstimate(flops=70_000_000, bytes_accessed=4_000_000, transcendentals=0),

time: 95.3 us -> 95.2 us (level)
  no operation moved by 1% of the time
where the time goes in v7:
time: 95.2 us; the launch traced here: 95.1 us
  Pallas kernels  94.4 us (99%)
    pallas_call x1, Pallas kernels, per_device(): pl.pallas_call(kernel, out_shape=(jax.ShapeDtypeStruct((NQ, NZ, 16, LANES...  90.9 us
    pallas_call x1, Pallas kernels, per_device(): pl.pallas_call(finish, out_shape=(jax.ShapeDtypeStruct(columns.shape, BF1...  3.5 us

profile of v7, /device:TPU:1, one launch (start us, length us, event | category | flops | bytes accessed | tf_op | source)
XLA Modules:
  0.0 95.1 jit_solution(18003605925150729624)
XLA Ops:
  0.6 90.9 %shard_map.85 = (bf16[8,16,16,128]{3,2,1,0:T(8,128)(2,1)}, bf16[256,1024]{1,0:T(8,128)(2,1)}, bf16[256,1024]{1,0:T(8,128)(2,1)}) custom-call(s32[1,128]{1,0:T(1,128)} %bitcast.7, bf16[2048,128]{1,0:T(8,128)(2,1)} %bitcast.9, bf16[256,1024]{1,0:T(8,128)(2,1)} %lf_in.1, bf16[256,1024]{1,0:T(8,128)(2,1)} %rf_in.1, bf16[256,1024]{1,0:T(8,128)(2,1)} %lr_in.1, ...), custom_call_target="tpu_custom_call" | custom-call | flops 2200000000 | bytes 8000000 | tf_op jit(solution)/shard_map/pallas_call | solution.py:384
  91.6 3.5 %shard_map.86 = (bf16[2048,128]{1,0:T(8,128)(2,1)}, bf16[256,1024]{1,0:T(8,128)(2,1)}, bf16[256,1024]{1,0:T(8,128)(2,1)}) custom-call(s32[1,128]{1,0:T(1,128)} %bitcast.8, bf16[8,16,16,128]{3,2,1,0:T(8,128)(2,1)} %get-tuple-element.9.final, bf16[256,1024]{1,0:T(8,128)(2,1)} %get-tuple-element.10.lnew, bf16[256,1024]{1,0:T(8,128)(2,1)} %get-tuple-element.11.rnew), custom_call_target="tpu_custom_call" | custom-call | flops 70000000 | bytes 4000000 | tf_op jit(solution)/shard_map/pallas_call | solution.py:426

commit v8 on v7

--- a/solution.py
+++ b/solution.py
@@ -79,8 +79,15 @@
         load.start()
     barrier = pltpu.get_barrier_semaphore()
 
+    def greet(fd):
+        pl.semaphore_signal(barrier, inc=1, device_id=(z, fd), device_id_type=MESH)
+
     def greet_plane(i, carry):
-        pl.semaphore_signal(barrier, inc=1, device_id=(z, (f + i) % NF), device_id_type=MESH)
+        greet((xy + i) % (NF // 2) * 2 + core)
+        return carry
+
+    def greet_back(i, carry):
+        greet(i * GROUP + x)
         return carry
 
     def greet_ring(i, carry):
@@ -88,7 +95,13 @@
         return carry
 
     lax.fori_loop(1, NZ, greet_ring, 0)
-    lax.fori_loop(1, NF, greet_plane, 0)
+    lax.fori_loop(1, NF // 2, greet_plane, 0)
+    greet(sibling)
+    greet(across + 1 - 2 * core)
+
+    @pl.when(x % 2 != core)
+    def _():
+        lax.fori_loop(0, NQ, greet_back, 0)
 
     owner = owner_ref[...]
     slot_row = lax.broadcasted_iota(jnp.int32, (LANES, LANES), 0)
@@ -100,7 +113,7 @@
     for zd in range(NZ):
         send_fwd[zd] = wide[zd * 128 : zd * 128 + 128, :].reshape(NQ, 16, LANES).astype(BF16)
 
-    pl.semaphore_wait(barrier, NZ - 1 + NF - 1)
+    pl.semaphore_wait(barrier, NZ - 1 + NF // 2 - 1 + 2 + 4)
 
     way = 1 - 2 * core
 

time: 95.2 us -> 96.1 us (level); the launches traced: 95.1 us -> 94.8 us
  no operation moved by 1% of the time
where the time goes in v8:
time: 96.1 us; the launch traced here: 94.8 us
  Pallas kernels  94.1 us (98%)
    pallas_call x1, Pallas kernels, per_device(): pl.pallas_call(kernel, out_shape=(jax.ShapeDtypeStruct((NQ, NZ, 16, LANES...  90.6 us
    pallas_call x1, Pallas kernels, per_device(): pl.pallas_call(finish, out_shape=(jax.ShapeDtypeStruct(columns.shape, BF1...  3.5 us

profile of v8, /device:TPU:1, one launch (start us, length us, event | category | flops | bytes accessed | tf_op | source)
XLA Modules:
  0.0 94.8 jit_solution(5133554060537042613)
XLA Ops:
  0.6 90.6 %shard_map.85 = (bf16[8,16,16,128]{3,2,1,0:T(8,128)(2,1)}, bf16[256,1024]{1,0:T(8,128)(2,1)}, bf16[256,1024]{1,0:T(8,128)(2,1)}) custom-call(s32[1,128]{1,0:T(1,128)} %bitcast.7, bf16[2048,128]{1,0:T(8,128)(2,1)} %bitcast.9, bf16[256,1024]{1,0:T(8,128)(2,1)} %lf_in.1, bf16[256,1024]{1,0:T(8,128)(2,1)} %rf_in.1, bf16[256,1024]{1,0:T(8,128)(2,1)} %lr_in.1, ...), custom_call_target="tpu_custom_call" | custom-call | flops 2200000000 | bytes 8000000 | tf_op jit(solution)/shard_map/pallas_call | solution.py:397
  91.3 3.5 %shard_map.86 = (bf16[2048,128]{1,0:T(8,128)(2,1)}, bf16[256,1024]{1,0:T(8,128)(2,1)}, bf16[256,1024]{1,0:T(8,128)(2,1)}) custom-call(s32[1,128]{1,0:T(1,128)} %bitcast.8, bf16[8,16,16,128]{3,2,1,0:T(8,128)(2,1)} %get-tuple-element.9.final, bf16[256,1024]{1,0:T(8,128)(2,1)} %get-tuple-element.10.lnew, bf16[256,1024]{1,0:T(8,128)(2,1)} %get-tuple-element.11.rnew), custom_call_target="tpu_custom_call" | custom-call | flops 70000000 | bytes 4000000 | tf_op jit(solution)/shard_map/pallas_call | solution.py:439
